TPU v7x, 256 devices: a whole 4x4x8 slice. The times are simulated.
256 devices in a mesh: lat: 16 (over y, x_lo, core), lon: 16 (over z, x_hi).
Axes of the slice: x: 4 (x_hi: 2, x_lo: 2; x = x_hi * 2 + x_lo), y: 4, z: 8, core: 2. Of those that a mesh axis runs over, the one named last changes fastest.
Arguments:
- noise: float32 [4, 8, 256, 4096], P(None, None, 'lat', 'lon'), may hold values from -6 to 6
- diff_lat: float32 [8, 256, 4096], P(None, 'lat', 'lon'), may hold values from 0.05 to 0.24
- diff_lon: float32 [8, 256, 4096], P(None, 'lat', 'lon'), may hold values from 0.05 to 0.24
- shear: float32 [8, 256, 4096], P(None, 'lat', 'lon'), may hold values from -0.9 to 0.9
- sea_mask: int32 [8, 256, 4096], P(None, 'lat', 'lon'), may hold values from 0 to 1, as said below
Outputs:
- normalized: float32 [4, 8, 256, 4096], P(None, None, 'lat', 'lon')
- mean_var: float32 [], replicated
Inputs may be any that keep to these rules, and one draw needn't show every extreme that they name: `sea_mask`: every block of 16 latitude rows by 256 longitude columns has its own chance for each cell to be wet, from a quarter to one; the block of the first rows and first columns is wet at every level.
All inputs are finite; a program needn't handle non-finite values.
Results may differ from a plain program's by a relative error of at most 0.0003.
Values sent between devices are 32-bit elements; how exact they have to be, the bound alone decides.
A program may use at most 64 MiB of HBM per device.

v0:
```python
import jax
import jax.numpy as jnp
from jax import lax
from jax.sharding import PartitionSpec as P

SAMPLES = 4
ITERS = 4


def with_halo(x, sides, width, wrap):
    for axis, dim in sides:
        size, length = (lax.axis_size(axis), x.shape[dim])
        up = [(i, (i + 1) % size) for i in range(size if wrap else size - 1)]
        down = [(j, i) for i, j in up]
        last = lax.slice_in_dim(x, length - width, length, axis=dim)
        first = lax.slice_in_dim(x, 0, width, axis=dim)
        before = lax.ppermute(last, axis, up)
        after = lax.ppermute(first, axis, down)
        x = jnp.concatenate([before, x, after], axis=dim)
    return x


def widen(field, width):
    field = with_halo(field, (("lon", 3),), width, True)
    return with_halo(field, (("lat", 2),), width, False)


def adjoint_step(padded, tensors):
    height = padded.shape[2]
    breadth = padded.shape[3]
    k11 = tensors[0]
    k22 = tensors[1]
    cross = tensors[2] * jnp.sqrt(k11 * k22)
    masked = tensors[3] * padded
    table = [
        ((0, 0), 1.0 - 2.0 * (k11 + k22)),
        ((1, 0), k11),
        ((-1, 0), k11),
        ((0, 1), k22),
        ((0, -1), k22),
        ((1, 1), 0.5 * cross),
        ((-1, -1), 0.5 * cross),
        ((1, -1), -0.5 * cross),
        ((-1, 1), -0.5 * cross),
    ]
    total = jnp.zeros(padded.shape[:2] + (height - 2, breadth - 2), jnp.float32)
    for offset, weight in table:
        product = weight * masked
        total = (
            total
            + product[
                :,
                :,
                1 - offset[0] : height - 1 - offset[0],
                1 - offset[1] : breadth - 1 - offset[1],
            ]
        )
    return total


def shards(noise, diff_lat, diff_lon, shear, sea_mask):
    rows = noise.shape[2]
    cols = noise.shape[3]
    wet = sea_mask.astype(jnp.float32)
    stacked = jnp.stack([diff_lat, diff_lon, shear, wet], axis=0)
    wide_tensors = widen(stacked, ITERS)
    field = noise
    tensors = wide_tensors[:, :, ITERS - 1 : ITERS + rows + 1, ITERS - 1 : ITERS + cols + 1]
    for step in range(ITERS):
        field = adjoint_step(widen(field, 1), tensors)
    var = jnp.sum(field * field, axis=0) / SAMPLES
    wet_sum, wet_count = lax.psum((jnp.sum(wet * var), jnp.sum(wet)), ("lat", "lon"))
    mean_var = wet_sum / wet_count
    safe = jnp.where(wet > 0, var, 1.0)
    factor = wet * jnp.sqrt(mean_var / (safe + 1e-06))
    return (field * factor, mean_var)


def solution(mesh):
    return jax.shard_map(
        shards,
        mesh=mesh,
        in_specs=(
            P(None, None, "lat", "lon"),
            P(None, "lat", "lon"),
            P(None, "lat", "lon"),
            P(None, "lat", "lon"),
            P(None, "lat", "lon"),
        ),
        out_specs=(P(None, None, "lat", "lon"), P()),
        check_vma=False,
    )
```

profile of v0, /device:TPU:1, one launch (start us, length us, event | category | flops | bytes accessed | tf_op | source)
XLA Modules:
  0.0 215.4 jit_solution(6304055585549230005)
XLA Ops:
  2.9 3.7 %collective-permute-start = (f32[4,8,16,4]{3,2,1,0:T(8,128)S(1)}, f32[4,8,16,4]{3,2,1,0:T(8,128)S(1)}, u32[]{:S(2)}, u32[]{:S(2)}) collective-permute-start(f32[4,8,16,4]{3,2,1,0:T(8,128)S(1)} %get-tuple-element.52), channel_id=1, source_target_pairs={{0,1},{1,2},{2,3},{3,4},{4,5},{5,6},{6,7},{7,8},{8,9},{9,10},{10,1... | collective-permute-start | bytes 24584 | tf_op jit(solution)/shard_map/ppermute | solution.py:17
  6.5 5.4 %collective-permute-start.1 = (f32[4,8,16,4]{3,2,1,0:T(8,128)S(1)}, f32[4,8,16,4]{3,2,1,0:T(8,128)S(1)}, u32[]{:S(2)}, u32[]{:S(2)}) collective-permute-start(f32[4,8,16,4]{3,2,1,0:T(8,128)S(1)} %get-tuple-element.53), channel_id=1, source_target_pairs={{1,0},{2,1},{3,2},{4,3},{5,4},{6,5},{7,6},{8,7},{9,8},{10,9},{11,1... | collective-permute-start | bytes 24584 | tf_op jit(solution)/shard_map/ppermute | solution.py:18
  11.9 6.0 %collective-permute-done = f32[4,8,16,4]{3,2,1,0:T(8,128)S(1)} collective-permute-done((f32[4,8,16,4]{3,2,1,0:T(8,128)S(1)}, f32[4,8,16,4]{3,2,1,0:T(8,128)S(1)}, u32[]{:S(2)}, u32[]{:S(2)}) %collective-permute-start) | collective-permute-done | bytes 8224 | tf_op jit(solution)/shard_map/ppermute | solution.py:17
  20.8 4.0 %collective-permute-start.2 = (f32[4,8,4,264]{3,2,1,0:T(4,128)S(1)}, f32[4,8,4,264]{3,2,1,0:T(4,128)S(1)}, u32[]{:S(2)}, u32[]{:S(2)}) collective-permute-start(f32[4,8,4,264]{3,2,1,0:T(4,128)S(1)} %get-tuple-element.42), channel_id=1, source_target_pairs={{0,16},{16,32},{32,48},{48,64},{64,80},{80,96},{96,112},{112,128},... | collective-permute-start | bytes 405512 | tf_op jit(solution)/shard_map/ppermute | solution.py:17
  27.6 5.4 %collective-permute-start.5 = (f32[4,8,16,1]{3,2,1,0:T(8,128)S(1)}, f32[4,8,16,1]{3,2,1,0:T(8,128)S(1)}, u32[]{:S(2)}, u32[]{:S(2)}) collective-permute-start(f32[4,8,16,1]{3,2,1,0:T(8,128)S(1)} %get-tuple-element.51), channel_id=1, source_target_pairs={{1,0},{2,1},{3,2},{4,3},{5,4},{6,5},{7,6},{8,7},{9,8},{10,9},{11,1... | collective-permute-start | bytes 6152 | tf_op jit(solution)/shard_map/ppermute | solution.py:18
  33.0 5.7 %collective-permute-done.4 = f32[4,8,16,1]{3,2,1,0:T(8,128)S(1)} collective-permute-done((f32[4,8,16,1]{3,2,1,0:T(8,128)S(1)}, f32[4,8,16,1]{3,2,1,0:T(8,128)S(1)}, u32[]{:S(2)}, u32[]{:S(2)}) %collective-permute-start.4) | collective-permute-done | bytes 2080 | tf_op jit(solution)/shard_map/ppermute | solution.py:17
  38.6 2.8 %collective-permute-done.5 = f32[4,8,16,1]{3,2,1,0:T(8,128)S(1)} collective-permute-done((f32[4,8,16,1]{3,2,1,0:T(8,128)S(1)}, f32[4,8,16,1]{3,2,1,0:T(8,128)S(1)}, u32[]{:S(2)}, u32[]{:S(2)}) %collective-permute-start.5) | collective-permute-done | bytes 2080 | tf_op jit(solution)/shard_map/ppermute | solution.py:18
  41.8 5.4 %collective-permute-start.6 = (f32[4,8,1,258]{3,2,1,0:T(1,128)S(1)}, f32[4,8,1,258]{3,2,1,0:T(1,128)S(1)}, u32[]{:S(2)}, u32[]{:S(2)}) collective-permute-start(f32[4,8,1,258]{3,2,1,0:T(1,128)S(1)} %get-tuple-element.40), channel_id=1, source_target_pairs={{0,16},{16,32},{32,48},{48,64},{64,80},{80,96},{96,112},{112,128},... | collective-permute-start | bytes 99080 | tf_op jit(solution)/shard_map/ppermute | solution.py:17
  54.6 2.6 %collective-permute-start.8 = (f32[4,8,16,1]{3,2,1,0:T(8,128)S(1)}, f32[4,8,16,1]{3,2,1,0:T(8,128)S(1)}, u32[]{:S(2)}, u32[]{:S(2)}) collective-permute-start(f32[4,8,16,1]{3,2,1,0:T(8,128)S(1)} %get-tuple-element.48), channel_id=1, source_target_pairs={{0,1},{1,2},{2,3},{3,4},{4,5},{5,6},{6,7},{7,8},{8,9},{9,10},{10,1... | collective-permute-start | bytes 6152 | tf_op jit(solution)/shard_map/ppermute | solution.py:17
  57.2 4.1 %collective-permute-start.9 = (f32[4,8,16,1]{3,2,1,0:T(8,128)S(1)}, f32[4,8,16,1]{3,2,1,0:T(8,128)S(1)}, u32[]{:S(2)}, u32[]{:S(2)}) collective-permute-start(f32[4,8,16,1]{3,2,1,0:T(8,128)S(1)} %get-tuple-element.49), channel_id=1, source_target_pairs={{1,0},{2,1},{3,2},{4,3},{5,4},{6,5},{7,6},{8,7},{9,8},{10,9},{11,1... | collective-permute-start | bytes 6152 | tf_op jit(solution)/shard_map/ppermute | solution.py:18
  61.3 5.8 %collective-permute-done.8 = f32[4,8,16,1]{3,2,1,0:T(8,128)S(1)} collective-permute-done((f32[4,8,16,1]{3,2,1,0:T(8,128)S(1)}, f32[4,8,16,1]{3,2,1,0:T(8,128)S(1)}, u32[]{:S(2)}, u32[]{:S(2)}) %collective-permute-start.8) | collective-permute-done | bytes 2080 | tf_op jit(solution)/shard_map/ppermute | solution.py:17
  67.1 3.7 %collective-permute-done.9 = f32[4,8,16,1]{3,2,1,0:T(8,128)S(1)} collective-permute-done((f32[4,8,16,1]{3,2,1,0:T(8,128)S(1)}, f32[4,8,16,1]{3,2,1,0:T(8,128)S(1)}, u32[]{:S(2)}, u32[]{:S(2)}) %collective-permute-start.9) | collective-permute-done | bytes 2080 | tf_op jit(solution)/shard_map/ppermute | solution.py:18
  71.2 3.6 %collective-permute-start.10 = (f32[4,8,1,258]{3,2,1,0:T(1,128)S(1)}, f32[4,8,1,258]{3,2,1,0:T(1,128)S(1)}, u32[]{:S(2)}, u32[]{:S(2)}) collective-permute-start(f32[4,8,1,258]{3,2,1,0:T(1,128)S(1)} %get-tuple-element.38), channel_id=1, source_target_pairs={{0,16},{16,32},{32,48},{48,64},{64,80},{80,96},{96,112},{112,128},... | collective-permute-start | bytes 99080 | tf_op jit(solution)/shard_map/ppermute | solution.py:17
  76.7 3.5 %collective-permute-done.11 = f32[4,8,1,258]{3,2,1,0:T(1,128)S(1)} collective-permute-done((f32[4,8,1,258]{3,2,1,0:T(1,128)S(1)}, f32[4,8,1,258]{3,2,1,0:T(1,128)S(1)}, u32[]{:S(2)}, u32[]{:S(2)}) %collective-permute-start.11) | collective-permute-done | bytes 33056 | tf_op jit(solution)/shard_map/ppermute | solution.py:18
  82.5 4.8 %collective-permute-start.13 = (f32[4,8,16,1]{3,2,1,0:T(8,128)S(1)}, f32[4,8,16,1]{3,2,1,0:T(8,128)S(1)}, u32[]{:S(2)}, u32[]{:S(2)}) collective-permute-start(f32[4,8,16,1]{3,2,1,0:T(8,128)S(1)} %get-tuple-element.47), channel_id=1, source_target_pairs={{1,0},{2,1},{3,2},{4,3},{5,4},{6,5},{7,6},{8,7},{9,8},{10,9},{11,1... | collective-permute-start | bytes 6152 | tf_op jit(solution)/shard_map/ppermute | solution.py:18
  87.3 5.1 %collective-permute-done.12 = f32[4,8,16,1]{3,2,1,0:T(8,128)S(1)} collective-permute-done((f32[4,8,16,1]{3,2,1,0:T(8,128)S(1)}, f32[4,8,16,1]{3,2,1,0:T(8,128)S(1)}, u32[]{:S(2)}, u32[]{:S(2)}) %collective-permute-start.12) | collective-permute-done | bytes 2080 | tf_op jit(solution)/shard_map/ppermute | solution.py:17
  92.4 3.7 %collective-permute-done.13 = f32[4,8,16,1]{3,2,1,0:T(8,128)S(1)} collective-permute-done((f32[4,8,16,1]{3,2,1,0:T(8,128)S(1)}, f32[4,8,16,1]{3,2,1,0:T(8,128)S(1)}, u32[]{:S(2)}, u32[]{:S(2)}) %collective-permute-start.13) | collective-permute-done | bytes 2080 | tf_op jit(solution)/shard_map/ppermute | solution.py:18
  101.0 4.0 %collective-permute-done.15 = f32[4,8,1,258]{3,2,1,0:T(1,128)S(1)} collective-permute-done((f32[4,8,1,258]{3,2,1,0:T(1,128)S(1)}, f32[4,8,1,258]{3,2,1,0:T(1,128)S(1)}, u32[]{:S(2)}, u32[]{:S(2)}) %collective-permute-start.15) | collective-permute-done | bytes 33056 | tf_op jit(solution)/shard_map/ppermute | solution.py:18
  107.0 5.1 %collective-permute-start.17 = (f32[4,8,16,1]{3,2,1,0:T(8,128)S(1)}, f32[4,8,16,1]{3,2,1,0:T(8,128)S(1)}, u32[]{:S(2)}, u32[]{:S(2)}) collective-permute-start(f32[4,8,16,1]{3,2,1,0:T(8,128)S(1)} %get-tuple-element.45), channel_id=1, source_target_pairs={{1,0},{2,1},{3,2},{4,3},{5,4},{6,5},{7,6},{8,7},{9,8},{10,9},{11,1... | collective-permute-start | bytes 6152 | tf_op jit(solution)/shard_map/ppermute | solution.py:18
  112.0 4.4 %collective-permute-done.16 = f32[4,8,16,1]{3,2,1,0:T(8,128)S(1)} collective-permute-done((f32[4,8,16,1]{3,2,1,0:T(8,128)S(1)}, f32[4,8,16,1]{3,2,1,0:T(8,128)S(1)}, u32[]{:S(2)}, u32[]{:S(2)}) %collective-permute-start.16) | collective-permute-done | bytes 2080 | tf_op jit(solution)/shard_map/ppermute | solution.py:17
  116.4 5.7 %collective-permute-done.17 = f32[4,8,16,1]{3,2,1,0:T(8,128)S(1)} collective-permute-done((f32[4,8,16,1]{3,2,1,0:T(8,128)S(1)}, f32[4,8,16,1]{3,2,1,0:T(8,128)S(1)}, u32[]{:S(2)}, u32[]{:S(2)}) %collective-permute-start.17) | collective-permute-done | bytes 2080 | tf_op jit(solution)/shard_map/ppermute | solution.py:18
  122.4 3.6 %collective-permute-start.18 = (f32[4,8,1,258]{3,2,1,0:T(1,128)S(1)}, f32[4,8,1,258]{3,2,1,0:T(1,128)S(1)}, u32[]{:S(2)}, u32[]{:S(2)}) collective-permute-start(f32[4,8,1,258]{3,2,1,0:T(1,128)S(1)} %get-tuple-element.34), channel_id=1, source_target_pairs={{0,16},{16,32},{32,48},{48,64},{64,80},{80,96},{96,112},{112,128},... | collective-permute-start | bytes 99080 | tf_op jit(solution)/shard_map/ppermute | solution.py:17
  128.0 3.5 %collective-permute-done.19 = f32[4,8,1,258]{3,2,1,0:T(1,128)S(1)} collective-permute-done((f32[4,8,1,258]{3,2,1,0:T(1,128)S(1)}, f32[4,8,1,258]{3,2,1,0:T(1,128)S(1)}, u32[]{:S(2)}, u32[]{:S(2)}) %collective-permute-start.19) | collective-permute-done | bytes 33056 | tf_op jit(solution)/shard_map/ppermute | solution.py:18
  133.9 78.0 %all-reduce = (f32[]{:T(128)}, f32[]{:T(128)}) all-reduce(f32[]{:T(128)} %get-tuple-element.3, f32[]{:T(128)} %get-tuple-element.2), channel_id=1, replica_groups=mesh['lat'=16,'lon'=16] {'lat','lon'}, use_global_device_ids=true, to_apply=%region_2.0 | all-reduce | flops 2 | bytes 16 | tf_op jit(solution)/shard_map/psum | solution.py:72
  (57 shorter events, 32.5 us)
Async XLA Ops:
  0.6 19.9 %copy-start.2 = (f32[8,16,256]{2,1,0:T(8,128)S(1)}, f32[8,16,256]{2,1,0:T(8,128)}, u32[]{:S(2)}) copy-start(f32[8,16,256]{2,1,0:T(8,128)} %param.8) | copy-start | bytes 393220
  0.6 19.8 %copy-start.3 = (f32[8,16,256]{2,1,0:T(8,128)S(1)}, f32[8,16,256]{2,1,0:T(8,128)}, u32[]{:S(2)}) copy-start(f32[8,16,256]{2,1,0:T(8,128)} %param.7) | copy-start | bytes 393220
  0.7 19.8 %copy-start.4 = (f32[8,16,256]{2,1,0:T(8,128)S(1)}, f32[8,16,256]{2,1,0:T(8,128)}, u32[]{:S(2)}) copy-start(f32[8,16,256]{2,1,0:T(8,128)} %param.6) | copy-start | bytes 393220
  2.7 24.0 %copy-start = (f32[4,8,16,256]{3,2,1,0:T(8,128)S(1)}, f32[4,8,16,256]{3,2,1,0:T(8,128)}, u32[]{:S(2)}) copy-start(f32[4,8,16,256]{3,2,1,0:T(8,128)} %param.5) | copy-start | bytes 1572868
  2.9 15.0 %collective-permute-start = (f32[4,8,16,4]{3,2,1,0:T(8,128)S(1)}, f32[4,8,16,4]{3,2,1,0:T(8,128)S(1)}, u32[]{:S(2)}, u32[]{:S(2)}) collective-permute-start(f32[4,8,16,4]{3,2,1,0:T(8,128)S(1)} %get-tuple-element.52), channel_id=1, source_target_pairs={{0,1},{1,2},{2,3},{3,4},{4,5},{5,6},{6,7},{7,8},{8,9},{9,10},{10,1... | collective-permute-start | bytes 24584 | tf_op jit(solution)/shard_map/ppermute | solution.py:17
  6.5 14.0 %collective-permute-start.1 = (f32[4,8,16,4]{3,2,1,0:T(8,128)S(1)}, f32[4,8,16,4]{3,2,1,0:T(8,128)S(1)}, u32[]{:S(2)}, u32[]{:S(2)}) collective-permute-start(f32[4,8,16,4]{3,2,1,0:T(8,128)S(1)} %get-tuple-element.53), channel_id=1, source_target_pairs={{1,0},{2,1},{3,2},{4,3},{5,4},{6,5},{7,6},{8,7},{9,8},{10,9},{11,1... | collective-permute-start | bytes 24584 | tf_op jit(solution)/shard_map/ppermute | solution.py:18
  20.8 28.3 %collective-permute-start.2 = (f32[4,8,4,264]{3,2,1,0:T(4,128)S(1)}, f32[4,8,4,264]{3,2,1,0:T(4,128)S(1)}, u32[]{:S(2)}, u32[]{:S(2)}) collective-permute-start(f32[4,8,4,264]{3,2,1,0:T(4,128)S(1)} %get-tuple-element.42), channel_id=1, source_target_pairs={{0,16},{16,32},{32,48},{48,64},{64,80},{80,96},{96,112},{112,128},... | collective-permute-start | bytes 405512 | tf_op jit(solution)/shard_map/ppermute | solution.py:17
  24.8 24.3 %collective-permute-start.3 = (f32[4,8,4,264]{3,2,1,0:T(4,128)S(1)}, f32[4,8,4,264]{3,2,1,0:T(4,128)S(1)}, u32[]{:S(2)}, u32[]{:S(2)}) collective-permute-start(f32[4,8,4,264]{3,2,1,0:T(4,128)S(1)} %get-tuple-element.43), channel_id=1, source_target_pairs={{16,0},{32,16},{48,32},{64,48},{80,64},{96,80},{112,96},{128,112},... | collective-permute-start | bytes 405512 | tf_op jit(solution)/shard_map/ppermute | solution.py:18
  26.9 11.8 %collective-permute-start.4 = (f32[4,8,16,1]{3,2,1,0:T(8,128)S(1)}, f32[4,8,16,1]{3,2,1,0:T(8,128)S(1)}, u32[]{:S(2)}, u32[]{:S(2)}) collective-permute-start(f32[4,8,16,1]{3,2,1,0:T(8,128)S(1)} %get-tuple-element.50), channel_id=1, source_target_pairs={{0,1},{1,2},{2,3},{3,4},{4,5},{5,6},{6,7},{7,8},{8,9},{9,10},{10,1... | collective-permute-start | bytes 6152 | tf_op jit(solution)/shard_map/ppermute | solution.py:17
  27.6 13.9 %collective-permute-start.5 = (f32[4,8,16,1]{3,2,1,0:T(8,128)S(1)}, f32[4,8,16,1]{3,2,1,0:T(8,128)S(1)}, u32[]{:S(2)}, u32[]{:S(2)}) collective-permute-start(f32[4,8,16,1]{3,2,1,0:T(8,128)S(1)} %get-tuple-element.51), channel_id=1, source_target_pairs={{1,0},{2,1},{3,2},{4,3},{5,4},{6,5},{7,6},{8,7},{9,8},{10,9},{11,1... | collective-permute-start | bytes 6152 | tf_op jit(solution)/shard_map/ppermute | solution.py:18
  41.8 8.4 %collective-permute-start.6 = (f32[4,8,1,258]{3,2,1,0:T(1,128)S(1)}, f32[4,8,1,258]{3,2,1,0:T(1,128)S(1)}, u32[]{:S(2)}, u32[]{:S(2)}) collective-permute-start(f32[4,8,1,258]{3,2,1,0:T(1,128)S(1)} %get-tuple-element.40), channel_id=1, source_target_pairs={{0,16},{16,32},{32,48},{48,64},{64,80},{80,96},{96,112},{112,128},... | collective-permute-start | bytes 99080 | tf_op jit(solution)/shard_map/ppermute | solution.py:17
  47.2 5.4 %collective-permute-start.7 = (f32[4,8,1,258]{3,2,1,0:T(1,128)S(1)}, f32[4,8,1,258]{3,2,1,0:T(1,128)S(1)}, u32[]{:S(2)}, u32[]{:S(2)}) collective-permute-start(f32[4,8,1,258]{3,2,1,0:T(1,128)S(1)} %get-tuple-element.41), channel_id=1, source_target_pairs={{16,0},{32,16},{48,32},{64,48},{80,64},{96,80},{112,96},{128,112},... | collective-permute-start | bytes 99080 | tf_op jit(solution)/shard_map/ppermute | solution.py:18
  54.6 12.6 %collective-permute-start.8 = (f32[4,8,16,1]{3,2,1,0:T(8,128)S(1)}, f32[4,8,16,1]{3,2,1,0:T(8,128)S(1)}, u32[]{:S(2)}, u32[]{:S(2)}) collective-permute-start(f32[4,8,16,1]{3,2,1,0:T(8,128)S(1)} %get-tuple-element.48), channel_id=1, source_target_pairs={{0,1},{1,2},{2,3},{3,4},{4,5},{5,6},{6,7},{7,8},{8,9},{9,10},{10,1... | collective-permute-start | bytes 6152 | tf_op jit(solution)/shard_map/ppermute | solution.py:17
  57.2 13.6 %collective-permute-start.9 = (f32[4,8,16,1]{3,2,1,0:T(8,128)S(1)}, f32[4,8,16,1]{3,2,1,0:T(8,128)S(1)}, u32[]{:S(2)}, u32[]{:S(2)}) collective-permute-start(f32[4,8,16,1]{3,2,1,0:T(8,128)S(1)} %get-tuple-element.49), channel_id=1, source_target_pairs={{1,0},{2,1},{3,2},{4,3},{5,4},{6,5},{7,6},{8,7},{9,8},{10,9},{11,1... | collective-permute-start | bytes 6152 | tf_op jit(solution)/shard_map/ppermute | solution.py:18
  71.2 5.6 %collective-permute-start.10 = (f32[4,8,1,258]{3,2,1,0:T(1,128)S(1)}, f32[4,8,1,258]{3,2,1,0:T(1,128)S(1)}, u32[]{:S(2)}, u32[]{:S(2)}) collective-permute-start(f32[4,8,1,258]{3,2,1,0:T(1,128)S(1)} %get-tuple-element.38), channel_id=1, source_target_pairs={{0,16},{16,32},{32,48},{48,64},{64,80},{80,96},{96,112},{112,128},... | collective-permute-start | bytes 99080 | tf_op jit(solution)/shard_map/ppermute | solution.py:17
  74.8 5.4 %collective-permute-start.11 = (f32[4,8,1,258]{3,2,1,0:T(1,128)S(1)}, f32[4,8,1,258]{3,2,1,0:T(1,128)S(1)}, u32[]{:S(2)}, u32[]{:S(2)}) collective-permute-start(f32[4,8,1,258]{3,2,1,0:T(1,128)S(1)} %get-tuple-element.39), channel_id=1, source_target_pairs={{16,0},{32,16},{48,32},{64,48},{80,64},{96,80},{112,96},{128,112},... | collective-permute-start | bytes 99080 | tf_op jit(solution)/shard_map/ppermute | solution.py:18
  82.1 10.3 %collective-permute-start.12 = (f32[4,8,16,1]{3,2,1,0:T(8,128)S(1)}, f32[4,8,16,1]{3,2,1,0:T(8,128)S(1)}, u32[]{:S(2)}, u32[]{:S(2)}) collective-permute-start(f32[4,8,16,1]{3,2,1,0:T(8,128)S(1)} %get-tuple-element.46), channel_id=1, source_target_pairs={{0,1},{1,2},{2,3},{3,4},{4,5},{5,6},{6,7},{7,8},{8,9},{9,10},{10,1... | collective-permute-start | bytes 6152 | tf_op jit(solution)/shard_map/ppermute | solution.py:17
  82.5 13.6 %collective-permute-start.13 = (f32[4,8,16,1]{3,2,1,0:T(8,128)S(1)}, f32[4,8,16,1]{3,2,1,0:T(8,128)S(1)}, u32[]{:S(2)}, u32[]{:S(2)}) collective-permute-start(f32[4,8,16,1]{3,2,1,0:T(8,128)S(1)} %get-tuple-element.47), channel_id=1, source_target_pairs={{1,0},{2,1},{3,2},{4,3},{5,4},{6,5},{7,6},{8,7},{9,8},{10,9},{11,1... | collective-permute-start | bytes 6152 | tf_op jit(solution)/shard_map/ppermute | solution.py:18
  96.4 4.5 %collective-permute-start.14 = (f32[4,8,1,258]{3,2,1,0:T(1,128)S(1)}, f32[4,8,1,258]{3,2,1,0:T(1,128)S(1)}, u32[]{:S(2)}, u32[]{:S(2)}) collective-permute-start(f32[4,8,1,258]{3,2,1,0:T(1,128)S(1)} %get-tuple-element.36), channel_id=1, source_target_pairs={{0,16},{16,32},{32,48},{48,64},{64,80},{80,96},{96,112},{112,128},... | collective-permute-start | bytes 99080 | tf_op jit(solution)/shard_map/ppermute | solution.py:17
  99.0 5.9 %collective-permute-start.15 = (f32[4,8,1,258]{3,2,1,0:T(1,128)S(1)}, f32[4,8,1,258]{3,2,1,0:T(1,128)S(1)}, u32[]{:S(2)}, u32[]{:S(2)}) collective-permute-start(f32[4,8,1,258]{3,2,1,0:T(1,128)S(1)} %get-tuple-element.37), channel_id=1, source_target_pairs={{16,0},{32,16},{48,32},{64,48},{80,64},{96,80},{112,96},{128,112},... | collective-permute-start | bytes 99080 | tf_op jit(solution)/shard_map/ppermute | solution.py:18
  106.9 9.5 %collective-permute-start.16 = (f32[4,8,16,1]{3,2,1,0:T(8,128)S(1)}, f32[4,8,16,1]{3,2,1,0:T(8,128)S(1)}, u32[]{:S(2)}, u32[]{:S(2)}) collective-permute-start(f32[4,8,16,1]{3,2,1,0:T(8,128)S(1)} %get-tuple-element.44), channel_id=1, source_target_pairs={{0,1},{1,2},{2,3},{3,4},{4,5},{5,6},{6,7},{7,8},{8,9},{9,10},{10,1... | collective-permute-start | bytes 6152 | tf_op jit(solution)/shard_map/ppermute | solution.py:17
  107.0 15.1 %collective-permute-start.17 = (f32[4,8,16,1]{3,2,1,0:T(8,128)S(1)}, f32[4,8,16,1]{3,2,1,0:T(8,128)S(1)}, u32[]{:S(2)}, u32[]{:S(2)}) collective-permute-start(f32[4,8,16,1]{3,2,1,0:T(8,128)S(1)} %get-tuple-element.45), channel_id=1, source_target_pairs={{1,0},{2,1},{3,2},{4,3},{5,4},{6,5},{7,6},{8,7},{9,8},{10,9},{11,1... | collective-permute-start | bytes 6152 | tf_op jit(solution)/shard_map/ppermute | solution.py:18
  122.4 5.6 %collective-permute-start.18 = (f32[4,8,1,258]{3,2,1,0:T(1,128)S(1)}, f32[4,8,1,258]{3,2,1,0:T(1,128)S(1)}, u32[]{:S(2)}, u32[]{:S(2)}) collective-permute-start(f32[4,8,1,258]{3,2,1,0:T(1,128)S(1)} %get-tuple-element.34), channel_id=1, source_target_pairs={{0,16},{16,32},{32,48},{48,64},{64,80},{80,96},{96,112},{112,128},... | collective-permute-start | bytes 99080 | tf_op jit(solution)/shard_map/ppermute | solution.py:17
  126.1 5.4 %collective-permute-start.19 = (f32[4,8,1,258]{3,2,1,0:T(1,128)S(1)}, f32[4,8,1,258]{3,2,1,0:T(1,128)S(1)}, u32[]{:S(2)}, u32[]{:S(2)}) collective-permute-start(f32[4,8,1,258]{3,2,1,0:T(1,128)S(1)} %get-tuple-element.35), channel_id=1, source_target_pairs={{16,0},{32,16},{48,32},{64,48},{80,64},{96,80},{112,96},{128,112},... | collective-permute-start | bytes 99080 | tf_op jit(solution)/shard_map/ppermute | solution.py:18
  (1 other events, 0.9 us)
where the time goes:
time: 216 us; the launch traced here: 215 us
  blocking collectives  78 us (36%)
  starting transfers between devices  61 us (28%)
  waiting for transfers between devices  58.8 us (27%)
  other arithmetic  13.4 us (6%)
  between operations  3.42 us (2%)
    psum x1, blocking collectives, shards(): lax.psum((jnp.sum(wet * var), jnp.sum(wet)), ('lat', 'lon'))  78 us
    ppermute x10, starting transfers between devices, with_halo(): after = lax.ppermute(first, axis, down)  34.4 us
    ppermute x10, waiting for transfers between devices, with_halo(): after = lax.ppermute(first, axis, down)  31.8 us
    ppermute x10, waiting for transfers between devices, with_halo(): before = lax.ppermute(last, axis, up)  27 us
    ppermute x10, starting transfers between devices, with_halo(): before = lax.ppermute(last, axis, up)  26.6 us
  transfers between devices with their start and end apart: 20, of which 14 were waited for; matrix products, arithmetic and copies ran while one was open for 1% of the time, Pallas kernels for 0%

commit v1 on v0

v1 whole, which is shorter than its diff:
```python
import functools

import jax
import jax.numpy as jnp
from jax import lax
from jax.experimental import pallas as pl
from jax.experimental.pallas import tpu as pltpu
from jax.sharding import PartitionSpec as P

SAMPLES = 4
LEVELS = 8
ITERS = 4
LANES = 128
MESH = pl.DeviceIdType.MESH


def kernel(
    n_lat, n_lon, rows, groups,
    noise, k_lat, k_lon, shear, sea,
    out, stat,
    raw, raw_k, raw_m, y, yh, a, ah, var, lon_tx, lon_rx, diag_tx, diag_rx, part, result,
    in_sem, out_sem, lat_tx_sem, lat_rx_sem, lon_tx_sem, lon_rx_sem, diag_tx_sem, diag_rx_sem, sum_tx_sem, sum_rx_sem,
):
    w = ITERS
    tall = rows + 2 * w
    ia, ib = lax.axis_index("lat"), lax.axis_index("lon")
    east, west = lax.rem(ib + 1, n_lon), lax.rem(ib + n_lon - 1, n_lon)
    has_north, has_south = ia > 0, ia < n_lat - 1
    lane = lax.broadcasted_iota(jnp.int32, (LEVELS, LANES), 1)

    def half(h):
        return pl.ds(h * LANES, LANES)

    loads = []
    for f, src in enumerate((k_lat, k_lon, shear)):
        for h in range(2):
            loads.append(pltpu.make_async_copy(src.at[:, half(h)], raw_k.at[f, h], in_sem.at[f, h]))
    for h in range(2):
        loads.append(pltpu.make_async_copy(sea.at[:, half(h)], raw_m.at[h], in_sem.at[3, h]))
    for s in range(SAMPLES):
        for h in range(2):
            loads.append(pltpu.make_async_copy(noise.at[s, :, half(h)], raw.at[s, h], in_sem.at[4 + s, h]))
    for c in loads:
        c.start()

    barrier = pltpu.get_barrier_semaphore()

    def greet(pa, pb):
        pl.semaphore_signal(barrier, inc=1, device_id=(pa, pb), device_id_type=MESH)

    @pl.when(has_north)
    def _():
        for pb in (west, east, ib):
            greet(ia - 1, pb)

    @pl.when(has_south)
    def _():
        for pb in (west, east, ib):
            greet(ia + 1, pb)

    greet(ia, west)
    greet(ia, east)
    for group in groups:
        for ma, mb in group[1:]:
            greet(lax.bitwise_xor(ia, ma), lax.bitwise_xor(ib, mb))

    for c in loads[:8]:
        c.wait()
    for r in range(rows):
        for h in range(2):
            at = pl.ds(r, LEVELS, stride=rows)
            m = raw_m[h, at, :].astype(jnp.float32)
            k11 = raw_k[0, h, at, :]
            k22 = raw_k[1, h, at, :]
            a1 = m * k11
            a2 = m * k22
            a[1, w + r, h] = a1
            a[2, w + r, h] = a2
            a[3, w + r, h] = (0.5 * m) * (raw_k[2, h, at, :] * jnp.sqrt(k11 * k22))
            a[0, w + r, h] = m - 2.0 * (a1 + a2)
    for c in loads[8:]:
        c.wait()
    for s in range(SAMPLES):
        for r in range(rows):
            for h in range(2):
                y[s, w + r, h] = raw[s, h, pl.ds(r, LEVELS, stride=rows), :]

    group_of = lax.shift_right_logical(lane, 2)

    def pack(pieces):
        packed = jnp.zeros((LEVELS, LANES), jnp.float32)
        for k, (value, shift) in enumerate(pieces):
            moved = pltpu.roll(value, (shift + 4 * k) % LANES, 1) if (shift + 4 * k) % LANES else value
            packed = jnp.where(group_of == k, moved, packed)
        return packed

    for side, (h, shift) in enumerate(((1, 4), (0, 0))):
        for v in range(2):
            lon_tx[side, v] = pack([(y[2 * v + k // rows, w + k % rows, h], shift) for k in range(2 * rows)])
        lon_tx[side, 2] = pack([(a[1 + k // rows, w + k % rows, h], shift) for k in range(2 * rows)])
        lon_tx[side, 3] = pack([(a[3, w + k, h], shift) for k in range(rows)])
        for end, first in enumerate((w, rows)):
            pieces = [(y[s, first + i, h], shift) for s in range(SAMPLES) for i in range(w)]
            pieces += [(a[1 + f, first + i, h], shift) for f in range(3) for i in range(w)]
            diag_tx[end, side] = pack(pieces)

    zero = jnp.zeros((LEVELS, LANES), jnp.float32)

    def clear(first, corner):
        for i in range(w):
            for h in range(2):
                for f in range(1, 4):
                    a[f, first + i, h] = zero
                for s in range(SAMPLES):
                    y[s, first + i, h] = zero
        for side in range(2):
            diag_rx[corner, side] = zero

    @pl.when(jnp.logical_not(has_north))
    def _():
        clear(0, 0)

    @pl.when(jnp.logical_not(has_south))
    def _():
        clear(w + rows, 1)

    n_sum = sum(len(group) - 1 for group in groups)
    pl.semaphore_wait(barrier, 2 + n_sum + 3 * has_north.astype(jnp.int32) + 3 * has_south.astype(jnp.int32))

    def remote(src, dst, tx, rx, pa, pb):
        return pltpu.make_async_remote_copy(
            src_ref=src, dst_ref=dst, send_sem=tx, recv_sem=rx, device_id=(pa, pb), device_id_type=MESH
        )

    lon_copies = [
        remote(lon_tx.at[side], lon_rx.at[side], lon_tx_sem.at[side], lon_rx_sem.at[side], ia, (east, west)[side])
        for side in range(2)
    ]
    pa_of = (ia - 1, ia + 1)
    diag_copies = [
        [
            remote(diag_tx.at[end, side], diag_rx.at[1 - end, side], diag_tx_sem.at[end, side], diag_rx_sem.at[1 - end, side], pa_of[end], (east, west)[side])
            for side in range(2)
        ]
        for end in range(2)
    ]

    def lat_copy(end, piece):
        mine = pl.ds((w, rows)[end], w)
        theirs = pl.ds((w + rows, 0)[end], w)
        tx, rx = lat_tx_sem.at[end, piece], lat_rx_sem.at[1 - end, piece]
        if piece == SAMPLES:
            src, dst = a.at[pl.ds(1, 3), mine], a.at[pl.ds(1, 3), theirs]
        else:
            src, dst = y.at[piece, mine], y.at[piece, theirs]
        return remote(src, dst, tx, rx, pa_of[end], ib)

    lat_copies = [[lat_copy(end, piece) for piece in range(SAMPLES + 1)] for end in range(2)]
    present = (has_north, has_south)

    for end in range(2):

        @pl.when(present[end])
        def _(end=end):
            for c in diag_copies[end]:
                c.start()

    for c in lon_copies:
        c.start()
    for end in range(2):

        @pl.when(present[end])
        def _(end=end):
            for piece in (SAMPLES, 0, 1, 2, 3):
                lat_copies[end][piece].start()

    for c in lon_copies:
        c.wait_recv()

    def unpack(from_west, from_east, k):
        e = pltpu.roll(from_east, (LANES - 4 * k) % LANES, 1) if k else from_east
        v = pltpu.roll(from_west, LANES - 4 - 4 * k, 1) if k < 31 else from_west
        return jnp.where(lane < 4, e, jnp.where(lane >= LANES - 4, v, 0.0))

    for v in range(2):
        fw, fe = lon_rx[0, v], lon_rx[1, v]
        for k in range(2 * rows):
            yh[2 * v + k // rows, w + k % rows] = unpack(fw, fe, k)
    fw, fe = lon_rx[0, 2], lon_rx[1, 2]
    for k in range(2 * rows):
        ah[1 + k // rows, w + k % rows] = unpack(fw, fe, k)
    fw, fe = lon_rx[0, 3], lon_rx[1, 3]
    for k in range(rows):
        ah[3, w + k] = unpack(fw, fe, k)
    for end in range(2):

        @pl.when(present[end])
        def _(end=end):
            for side in range(2):
                diag_copies[1 - end][side].wait_recv()

    for end, first in enumerate((0, w + rows)):
        fw, fe = diag_rx[end, 0], diag_rx[end, 1]
        k = 0
        for s in range(SAMPLES):
            for i in range(w):
                yh[s, first + i] = unpack(fw, fe, k)
                k += 1
        for f in range(3):
            for i in range(w):
                ah[1 + f, first + i] = unpack(fw, fe, k)
                k += 1

    for end in range(2):

        @pl.when(present[end])
        def _(end=end):
            lat_copies[1 - end][SAMPLES].wait_recv()

    def centre(a1, a2):
        return jnp.where(a1 > 0.0, 1.0, 0.0) - 2.0 * (a1 + a2)

    for e in range(tall):
        ah[0, e] = centre(ah[1, e], ah[2, e])
        if e < w or e >= w + rows:
            for h in range(2):
                a[0, e, h] = centre(a[1, e, h], a[2, e, h])
    for r in range(rows):
        for h in range(2):
            var[r, h] = zero

    first_lane, last_lane = lane == 0, lane == LANES - 1

    def diffuse(s):
        for t in range(1, ITERS + 1):
            last = t == ITERS

            def field(e, f):
                return [a[f, e, 0], a[f, e, 1], ah[f, e]]

            def products(e):
                z = [y[s, e, 0], y[s, e, 1], yh[s, e]]
                inside = t <= e < tall - t
                p1 = [u * v for u, v in zip(field(e, 1), z)]
                p3 = [u * v for u, v in zip(field(e, 3), z)]
                p0 = [u * v for u, v in zip(field(e, 0), z)] if inside else None
                p2 = [u * v for u, v in zip(field(e, 2), z)] if inside else None
                return p0, p1, p2, p3

            before, here = products(t - 1), products(t)
            for e in range(t, tall - t):
                after = products(e + 1)
                q = [u - v for u, v in zip(before[3], after[3])]
                left = [pltpu.roll(p + d, 1, 1) for p, d in zip(here[2], q)]
                right = [pltpu.roll(p - d, LANES - 1, 1) for p, d in zip(here[2], q)]
                for h in range(2 if last else 3):
                    total = here[0][h] + (before[1][h] + after[1][h])
                    total = total + jnp.where(first_lane, left[h - 1], left[h])
                    total = total + jnp.where(last_lane, right[(h + 1) % 3], right[h])
                    if h < 2:
                        y[s, e, h] = total
                    else:
                        yh[s, e] = total
                    if last:
                        var[e - w, h] += total * total
                before, here = here, after

    def sample(s, carry):
        for end in range(2):

            @pl.when(present[end])
            def _(end=end):
                mine, theirs = pl.ds((w, rows)[1 - end], w), pl.ds((w + rows, 0)[1 - end], w)
                remote(
                    y.at[s, mine], y.at[s, theirs], lat_tx_sem.at[1 - end, s], lat_rx_sem.at[end, s], pa_of[1 - end], ib
                ).wait_recv()
                remote(
                    y.at[s, theirs], y.at[s, theirs], lat_tx_sem.at[end, s], lat_rx_sem.at[end, s], pa_of[end], ib
                ).wait_send()

        diffuse(s)
        return carry

    lax.fori_loop(0, SAMPLES, sample, 0)

    total_v, total_m = zero, zero
    for r in range(rows):
        for h in range(2):
            wet = jnp.where(a[1, w + r, h] > 0.0, 1.0, 0.0)
            v = var[r, h] * (1.0 / SAMPLES)
            total_v = total_v + wet * v
            total_m = total_m + wet
            var[r, h] = wet * lax.rsqrt(jnp.where(wet > 0.0, v, 1.0) + 1e-06)

    row = lax.broadcasted_iota(jnp.int32, (LEVELS, LANES), 0)
    mine = jnp.where(row == 0, jnp.sum(total_v, axis=0, keepdims=True), jnp.sum(total_m, axis=0, keepdims=True))

    def rank(masks):
        out = 0
        for bit, (ma, mb) in enumerate(masks):
            hit = lax.bitwise_and(ia, ma) + lax.bitwise_and(ib, mb)
            out = out + jnp.where(hit > 0, 1 << bit, 0)
        return out

    def sums(phase, mine):
        group = groups[phase]
        size = len(group)
        me = rank([group[1 << i] for i in range(size.bit_length() - 1)])
        part[phase, me] = mine
        copies = []
        for m in range(1, size):
            ma, mb = group[m]
            there = lax.bitwise_xor(me, m)
            pa, pb = lax.bitwise_xor(ia, ma), lax.bitwise_xor(ib, mb)
            slot = part.at[phase, me, pl.ds(0, 2)]
            copies.append(remote(slot, slot, sum_tx_sem.at[phase, m], sum_rx_sem.at[phase, me], pa, pb))
            copies[-1].start()
        return me, copies

    def gather(phase, me, copies):
        size = len(groups[phase])
        for m in range(1, size):
            there = lax.bitwise_xor(me, m)
            slot = part.at[phase, there, pl.ds(0, 2)]
            remote(slot, slot, sum_tx_sem.at[phase, m], sum_rx_sem.at[phase, there], ia, ib).wait_recv()
        total = part[phase, 0, 0:2]
        for j in range(1, size):
            total = total + part[phase, j, 0:2]
        return total

    me0, sent0 = sums(0, mine)

    def scaled(s, carry):
        for r in range(rows):
            for h in range(2):
                raw[s, h, pl.ds(r, LEVELS, stride=rows), :] = y[s, w + r, h] * var[r, h]
        for h in range(2):
            pltpu.make_async_copy(raw.at[s, h], out.at[s, :, half(h)], out_sem.at[s, h]).start()
        return carry

    lax.fori_loop(0, SAMPLES, scaled, 0)
    total = gather(0, me0, sent0)
    me1, sent1 = sums(1, jnp.concatenate([total] * (LEVELS // 2), axis=0))
    for s in range(SAMPLES):
        for h in range(2):
            pltpu.make_async_copy(raw.at[s, h], out.at[s, :, half(h)], out_sem.at[s, h]).wait()
    total = gather(1, me1, sent1)
    both = jnp.sum(total, axis=1, keepdims=True)
    stat[...] = jnp.broadcast_to(both[0:1] / both[1:2], stat.shape)

    for c in lon_copies + sent0 + sent1:
        c.wait_send()
    for end in range(2):

        @pl.when(present[end])
        def _(end=end):
            for c in diag_copies[end] + [lat_copies[end][SAMPLES]]:
                c.wait_send()


def bits_of(n):
    return [1 << i for i in range(n.bit_length() - 1)]


def span(masks):
    out = [(0, 0)]
    for ma, mb in masks:
        out += [(x + ma, z + mb) for x, z in out]
    return out


def shards(n_lat, n_lon, noise, diff_lat, diff_lon, shear, sea_mask):
    samples, levels, rows, cols = noise.shape
    lat_bits, lon_bits = bits_of(n_lat), bits_of(n_lon)
    groups = (
        span([(b, 0) for b in lat_bits[:1]] + [(0, b) for b in lon_bits[1:]]),
        span([(b, 0) for b in lat_bits[1:]] + [(0, b) for b in lon_bits[:1]]),
    )
    size = max(len(g) for g in groups)
    tall = rows + 2 * ITERS
    flat = levels * rows
    f32 = jnp.float32
    anywhere = pl.BlockSpec(memory_space=pl.ANY)
    dma = pltpu.SemaphoreType.DMA
    field, stat = pl.pallas_call(
        functools.partial(kernel, n_lat, n_lon, rows, groups),
        out_shape=(
            jax.ShapeDtypeStruct((samples, flat, cols), f32),
            jax.ShapeDtypeStruct((1, LANES), f32),
        ),
        in_specs=[anywhere] * 5,
        out_specs=(anywhere, pl.BlockSpec(memory_space=pltpu.VMEM)),
        scratch_shapes=[
            pltpu.VMEM((samples, 2, flat, LANES), f32),
            pltpu.VMEM((3, 2, flat, LANES), f32),
            pltpu.VMEM((2, flat, LANES), jnp.int32),
            pltpu.VMEM((samples, tall, 2, levels, LANES), f32),
            pltpu.VMEM((samples, tall, levels, LANES), f32),
            pltpu.VMEM((4, tall, 2, levels, LANES), f32),
            pltpu.VMEM((4, tall, levels, LANES), f32),
            pltpu.VMEM((rows, 2, levels, LANES), f32),
            pltpu.VMEM((2, 4, levels, LANES), f32),
            pltpu.VMEM((2, 4, levels, LANES), f32),
            pltpu.VMEM((2, 2, levels, LANES), f32),
            pltpu.VMEM((2, 2, levels, LANES), f32),
            pltpu.VMEM((2, size, levels, LANES), f32),
            pltpu.VMEM((levels, LANES), f32),
            dma((8, 2)),
            dma((samples, 2)),
            dma((2, samples + 1)),
            dma((2, samples + 1)),
            dma((2,)),
            dma((2,)),
            dma((2, 2)),
            dma((2, 2)),
            dma((2, size)),
            dma((2, size)),
        ],
        compiler_params=pltpu.CompilerParams(
            collective_id=0, has_side_effects=True, vmem_limit_bytes=60 << 20
        ),
    )(
        noise.reshape(samples, flat, cols),
        diff_lat.reshape(flat, cols),
        diff_lon.reshape(flat, cols),
        shear.reshape(flat, cols),
        sea_mask.reshape(flat, cols),
    )
    mean_var = stat[0, 0]
    return ((field * jnp.sqrt(mean_var)).reshape(noise.shape), mean_var)


def solution(mesh):
    return jax.shard_map(
        functools.partial(shards, mesh.shape["lat"], mesh.shape["lon"]),
        mesh=mesh,
        in_specs=(
            P(None, None, "lat", "lon"),
            P(None, "lat", "lon"),
            P(None, "lat", "lon"),
            P(None, "lat", "lon"),
            P(None, "lat", "lon"),
        ),
        out_specs=(P(None, None, "lat", "lon"), P()),
        check_vma=False,
    )
```

time: 216 us -> 33.3 us (0.15)
  blocking collectives: 78 us -> 0 us
  starting transfers between devices: 61 us -> 0 us
  waiting for transfers between devices: 58.8 us -> 0 us
  Pallas kernels: 0 us -> 28.6 us
  other arithmetic: 13.4 us -> 1.88 us
    psum x1 -> x0, blocking collectives: 78 us -> none  [shards(): lax.psum((jnp.sum(wet * var), jnp.sum(wet)), ('lat', 'lon'))]
    ppermute x20 -> x0, starting transfers between devices: 61 us -> none  [the longest x10 34.4 us: with_halo(): after = lax.ppermute(first, axis, down)]
    ppermute x20 -> x0, waiting for transfers between devices: 58.8 us -> none  [the longest x10 31.8 us: with_halo(): after = lax.ppermute(first, axis, down)]
    pallas_call x0 -> x1, Pallas kernels: none -> 28.6 us  [shards(): pl.pallas_call(functools.partial(kernel, n_lat, n_lon, rows, groups), out...]
    mul x11 -> x1, other arithmetic: 4.9 us -> 1.88 us  [shards(): return ((field * jnp.sqrt(mean_var)).reshape(noise.shape), mean_var)]
    add x3 -> x0, other arithmetic: 2.7 us -> none  [adjoint_step(): total + product[:, :, 1 - offset[0]:height - 1 - offset[0], 1 - offset[1]...]
  transfers between devices with their start and end apart: 20 -> 0, of which waited for: 14 -> 0; matrix products, arithmetic and copies ran while one was open for 1% -> 0% of each run, Pallas kernels for 0% -> 0%
where the time goes in v1:
time: 33.3 us; the launch traced here: 33.1 us
  Pallas kernels  28.6 us (86%)
  between operations  1.89 us (6%)
  other arithmetic  1.88 us (6%)
  local copies, waits for them, and re-layouts  0.66 us (2%)
    pallas_call x1, Pallas kernels, shards(): pl.pallas_call(functools.partial(kernel, n_lat, n_lon, rows, groups), out...  28.6 us
    mul x1, other arithmetic, shards(): return ((field * jnp.sqrt(mean_var)).reshape(noise.shape), mean_var)  1.88 us

profile of v1, /device:TPU:1, one launch (start us, length us, event | category | flops | bytes accessed | tf_op | source)
XLA Modules:
  0.0 33.1 jit_solution(6084089943844178626)
XLA Ops:
  0.6 28.6 %shard_map.68 = (f32[4,128,256]{2,1,0:T(8,128)}, f32[1,128]{1,0:T(1,128)}) custom-call(f32[4,128,256]{2,1,0:T(8,128)} %bitcast.8, f32[128,256]{1,0:T(8,128)} %bitcast.10, f32[128,256]{1,0:T(8,128)} %bitcast.11, f32[128,256]{1,0:T(8,128)} %bitcast.12, s32[128,256]{1,0:T(8,128)} %bitcast.13), custom_call_target="tpu_custom_call" | custom-call | tf_op jit(solution)/shard_map/pallas_call | solution.py:385
  29.3 0.0 copy-start
  29.3 0.7 %copy-done = f32[1,128]{1,0:T(1,128)S(1)} copy-done((f32[1,128]{1,0:T(1,128)S(1)}, f32[1,128]{1,0:T(1,128)}, u32[]{:S(2)}) %copy-start) | copy-done | bytes 536
  30.0 1.9 %broadcast_multiply_fusion = f32[4,128,256]{2,1,0:T(8,128)} fusion(f32[4,128,256]{2,1,0:T(8,128)} %get-tuple-element.4, f32[]{:T(128)S(6)} %sqrt.3), kind=kLoop, calls=%fused_computation | loop fusion | flops 131072 | bytes 1048580 | tf_op jit(solution)/shard_map/mul | solution.py:430
Async XLA Ops:
  29.3 0.7 %copy-start = (f32[1,128]{1,0:T(1,128)S(1)}, f32[1,128]{1,0:T(1,128)}, u32[]{:S(2)}) copy-start(f32[1,128]{1,0:T(1,128)} %get-tuple-element.5) | copy-start | bytes 1540

commit v2 on v1

--- a/solution.py
+++ b/solution.py
@@ -19,7 +19,7 @@
     noise, k_lat, k_lon, shear, sea,
     out, stat,
     raw, raw_k, raw_m, y, yh, a, ah, var, lon_tx, lon_rx, diag_tx, diag_rx, part, result,
-    in_sem, out_sem, lat_tx_sem, lat_rx_sem, lon_tx_sem, lon_rx_sem, diag_tx_sem, diag_rx_sem, sum_tx_sem, sum_rx_sem,
+    in_sem, lat_tx_sem, lat_rx_sem, lon_tx_sem, lon_rx_sem, diag_tx_sem, diag_rx_sem, sum_tx_sem, sum_rx_sem,
 ):
     w = ITERS
     tall = rows + 2 * w
@@ -40,9 +40,6 @@
     for s in range(SAMPLES):
         for h in range(2):
             loads.append(pltpu.make_async_copy(noise.at[s, :, half(h)], raw.at[s, h], in_sem.at[4 + s, h]))
-    for c in loads:
-        c.start()
-
     barrier = pltpu.get_barrier_semaphore()
 
     def greet(pa, pb):
@@ -60,6 +57,8 @@
 
     greet(ia, west)
     greet(ia, east)
+    for c in loads:
+        c.start()
     for group in groups:
         for ma, mb in group[1:]:
             greet(lax.bitwise_xor(ia, ma), lax.bitwise_xor(ib, mb))
@@ -333,17 +332,12 @@
     def scaled(s, carry):
         for r in range(rows):
             for h in range(2):
-                raw[s, h, pl.ds(r, LEVELS, stride=rows), :] = y[s, w + r, h] * var[r, h]
-        for h in range(2):
-            pltpu.make_async_copy(raw.at[s, h], out.at[s, :, half(h)], out_sem.at[s, h]).start()
+                out[s, h, pl.ds(r, LEVELS, stride=rows), :] = y[s, w + r, h] * var[r, h]
         return carry
 
     lax.fori_loop(0, SAMPLES, scaled, 0)
     total = gather(0, me0, sent0)
     me1, sent1 = sums(1, jnp.concatenate([total] * (LEVELS // 2), axis=0))
-    for s in range(SAMPLES):
-        for h in range(2):
-            pltpu.make_async_copy(raw.at[s, h], out.at[s, :, half(h)], out_sem.at[s, h]).wait()
     total = gather(1, me1, sent1)
     both = jnp.sum(total, axis=1, keepdims=True)
     stat[...] = jnp.broadcast_to(both[0:1] / both[1:2], stat.shape)
@@ -356,6 +350,19 @@
         def _(end=end):
             for c in diag_copies[end] + [lat_copies[end][SAMPLES]]:
                 c.wait_send()
+
+
+def scale(field, stat, out, mean, buf, sem):
+    mean[...] = stat[...]
+    factor = jnp.sqrt(stat[...])
+    copies = []
+    for s in range(SAMPLES):
+        for h in range(2):
+            buf[s, h] = field[s, h] * factor
+            copies.append(pltpu.make_async_copy(buf.at[s, h], out.at[s, :, pl.ds(h * LANES, LANES)], sem.at[s, h]))
+            copies[-1].start()
+    for c in copies:
+        c.wait()
 
 
 def bits_of(n):
@@ -380,16 +387,17 @@
     tall = rows + 2 * ITERS
     flat = levels * rows
     f32 = jnp.float32
-    anywhere = pl.BlockSpec(memory_space=pl.ANY)
     dma = pltpu.SemaphoreType.DMA
+    hbm = pl.BlockSpec(memory_space=pltpu.HBM)
+    vmem = pl.BlockSpec(memory_space=pltpu.VMEM)
     field, stat = pl.pallas_call(
         functools.partial(kernel, n_lat, n_lon, rows, groups),
         out_shape=(
-            jax.ShapeDtypeStruct((samples, flat, cols), f32),
-            jax.ShapeDtypeStruct((1, LANES), f32),
+            pltpu.VMEM((samples, 2, flat, LANES), f32),
+            pltpu.VMEM((1, LANES), f32),
         ),
-        in_specs=[anywhere] * 5,
-        out_specs=(anywhere, pl.BlockSpec(memory_space=pltpu.VMEM)),
+        in_specs=[hbm] * 5,
+        out_specs=(vmem, vmem),
         scratch_shapes=[
             pltpu.VMEM((samples, 2, flat, LANES), f32),
             pltpu.VMEM((3, 2, flat, LANES), f32),
@@ -406,7 +414,6 @@
             pltpu.VMEM((2, size, levels, LANES), f32),
             pltpu.VMEM((levels, LANES), f32),
             dma((8, 2)),
-            dma((samples, 2)),
             dma((2, samples + 1)),
             dma((2, samples + 1)),
             dma((2,)),
@@ -426,8 +433,15 @@
         shear.reshape(flat, cols),
         sea_mask.reshape(flat, cols),
     )
-    mean_var = stat[0, 0]
-    return ((field * jnp.sqrt(mean_var)).reshape(noise.shape), mean_var)
+    out, mean_var = pl.pallas_call(
+        scale,
+        out_shape=(jax.ShapeDtypeStruct((samples, flat, cols), f32), jax.ShapeDtypeStruct((1, LANES), f32)),
+        in_specs=[vmem, vmem],
+        out_specs=(hbm, vmem),
+        scratch_shapes=[pltpu.VMEM((samples, 2, flat, LANES), f32), dma((samples, 2))],
+        compiler_params=pltpu.CompilerParams(vmem_limit_bytes=8 << 20),
+    )(pltpu.with_memory_space_constraint(field, pltpu.VMEM), pltpu.with_memory_space_constraint(stat, pltpu.VMEM))
+    return out.reshape(noise.shape), mean_var[0, 0]
 
 
 def solution(mesh):

time: 33.3 us -> 30.1 us (0.904)
  other arithmetic: 1.88 us -> 0 us
  between operations: 1.89 us -> 0.64 us
  Pallas kernels: 28.6 us -> 29.4 us
  local copies, waits for them, and re-layouts: 0.66 us -> 0 us
    mul x1 -> x0, other arithmetic: 1.88 us -> none  [shards(): return ((field * jnp.sqrt(mean_var)).reshape(noise.shape), mean_var)]
    pallas_call x0 -> x1, Pallas kernels: none -> 1.37 us  [shards(): pl.pallas_call(scale, out_shape=(jax.ShapeDtypeStruct((samples, flat, col...]
    unnamed x2 -> x0, local copies, waits for them, and re-layouts: 0.66 us -> none
    pallas_call x1, Pallas kernels: 28.6 us -> 28 us  [shards(): pl.pallas_call(functools.partial(kernel, n_lat, n_lon, rows, groups), out...]
where the time goes in v2:
time: 30.1 us; the launch traced here: 30 us
  Pallas kernels  29.4 us (98%)
  between operations  0.64 us (2%)
    pallas_call x1, Pallas kernels, shards(): pl.pallas_call(functools.partial(kernel, n_lat, n_lon, rows, groups), out...  28 us
    pallas_call x1, Pallas kernels, shards(): pl.pallas_call(scale, out_shape=(jax.ShapeDtypeStruct((samples, flat, col...  1.37 us

profile of v2, /device:TPU:1, one launch (start us, length us, event | category | flops | bytes accessed | tf_op | source)
XLA Modules:
  0.0 30.0 jit_solution(17901805421659332237)
XLA Ops:
  0.6 28.0 %shard_map.68 = (f32[4,2,128,128]{3,2,1,0:T(8,128)S(1)}, f32[1,128]{1,0:T(1,128)S(1)}) custom-call(f32[4,128,256]{2,1,0:T(8,128)} %bitcast.8, f32[128,256]{1,0:T(8,128)} %bitcast.9, f32[128,256]{1,0:T(8,128)} %bitcast.10, f32[128,256]{1,0:T(8,128)} %bitcast.11, s32[128,256]{1,0:T(8,128)} %bitcast.12), custom_call_target="tpu_custom_call" | custom-call | tf_op jit(solution)/shard_map/pallas_call | solution.py:393
  28.6 1.4 %shard_map.69 = (f32[4,128,256]{2,1,0:T(8,128)}, f32[1,128]{1,0:T(1,128)}) custom-call(f32[4,2,128,128]{3,2,1,0:T(8,128)S(1)} %get-tuple-element.6.field, f32[1,128]{1,0:T(1,128)S(1)} %get-tuple-element.7.stat), custom_call_target="tpu_custom_call" | custom-call | tf_op jit(solution)/shard_map/pallas_call | solution.py:436

commit v3 on v2

v3 whole, which is shorter than its diff:
```python
import functools

import jax
import jax.numpy as jnp
from jax import lax
from jax.experimental import pallas as pl
from jax.experimental.pallas import tpu as pltpu
from jax.sharding import PartitionSpec as P

SAMPLES = 4
LEVELS = 8
ITERS = 4
LANES = 128
MESH = pl.DeviceIdType.MESH


def kernel(
    n_lat, n_lon, rows, groups,
    noise, k_lat, k_lon, shear, sea,
    out, stat,
    raw, raw_k, raw_m, x, a, edge_tx, edge_rx, k_tx, k_rx, k_mid, corner_tx, corner_rx, hx, ha, lon_tx, lon_rx, diag_tx, diag_rx, xs, var, part,
    in_sem, lat_tx_sem, lat_rx_sem, lon_tx_sem, lon_rx_sem, diag_tx_sem, diag_rx_sem, sum_tx_sem, sum_rx_sem,
):
    w = ITERS
    tall = rows + 2 * w
    ia, ib = lax.axis_index("lat"), lax.axis_index("lon")
    east, west = lax.rem(ib + 1, n_lon), lax.rem(ib + n_lon - 1, n_lon)
    has_north, has_south = ia > 0, ia < n_lat - 1
    present = (has_north, has_south)
    pa_of = (ia - 1, ia + 1)
    lane = lax.broadcasted_iota(jnp.int32, (LEVELS, LANES), 1)
    zero = jnp.zeros((LEVELS, LANES), jnp.float32)

    def half(h):
        return pl.ds(h * LANES, LANES)

    loads = []
    for f, src in enumerate((k_lat, k_lon, shear)):
        for h in range(2):
            loads.append(pltpu.make_async_copy(src.at[:, half(h)], raw_k.at[f, h], in_sem.at[f, h]))
    for h in range(2):
        loads.append(pltpu.make_async_copy(sea.at[:, half(h)], raw_m.at[h], in_sem.at[3, h]))
    for s in range(SAMPLES):
        for h in range(2):
            loads.append(pltpu.make_async_copy(noise.at[s, :, half(h)], raw.at[s, h], in_sem.at[4 + s, h]))

    barrier = pltpu.get_barrier_semaphore()

    def greet(pa, pb):
        pl.semaphore_signal(barrier, inc=1, device_id=(pa, pb), device_id_type=MESH)

    for end in range(2):

        @pl.when(present[end])
        def _(end=end):
            for pb in (west, east, ib):
                greet(pa_of[end], pb)

    greet(ia, west)
    greet(ia, east)
    for c in loads:
        c.start()
    for group in groups:
        for ma, mb in group[1:]:
            greet(lax.bitwise_xor(ia, ma), lax.bitwise_xor(ib, mb))

    for c in loads[:8]:
        c.wait()
    for r in range(rows):
        for h in range(2):
            at = pl.ds(r, LEVELS, stride=rows)
            m = raw_m[h, at, :].astype(jnp.float32)
            k11 = raw_k[0, h, at, :]
            k22 = raw_k[1, h, at, :]
            a1 = m * k11
            a2 = m * k22
            a[1, r, h] = a1
            a[2, r, h] = a2
            a[3, r, h] = (0.5 * m) * (raw_k[2, h, at, :] * jnp.sqrt(k11 * k22))
            a[0, r, h] = m - 2.0 * (a1 + a2)

    place = lax.bitwise_and(lane, 31)
    sample_of = lax.shift_right_logical(lane, 5)
    low_own = jnp.logical_and(place >= 4, place < 16)
    high_own = jnp.logical_and(place >= 16, place < 28)

    def rolled(value, shift):
        shift %= LANES
        return pltpu.roll(value, shift, 1) if shift else value

    def replicate(value):
        value = value + pltpu.roll(value, 32, 1)
        return value + pltpu.roll(value, 64, 1)

    for f in range(1, 4):
        for r in range(rows):
            low = jnp.where(jnp.logical_and(low_own, lane < 32), rolled(a[f, r, 0], 4), 0.0)
            high = jnp.where(jnp.logical_and(high_own, lane < 32), rolled(a[f, r, 1], 28), low)
            ha[f, w + r] = replicate(high)

    for c in loads[8:]:
        c.wait()
    for s in range(SAMPLES):
        for r in range(rows):
            for h in range(2):
                x[0, s, r, h] = raw[s, h, pl.ds(r, LEVELS, stride=rows), :]
    for r in range(rows):
        side = zero
        for s in range(SAMPLES):
            mine = sample_of == s
            side = jnp.where(jnp.logical_and(low_own, mine), rolled(x[0, s, r, 0], 32 * s + 4), side)
            side = jnp.where(jnp.logical_and(high_own, mine), rolled(x[0, s, r, 1], 32 * s + 28), side)
        hx[0, w + r] = side

    offset = (24, 4)
    fours = lax.shift_right_logical(lane, 2)
    in_sample = lax.bitwise_and(fours, 7)
    for side in range(2):
        for v in range(2):
            packed, packed_k = zero, zero
            for j in range(8):
                e = w + 8 * v + j
                packed = jnp.where(in_sample == j, rolled(hx[0, e], 4 * j - offset[side]), packed)
                for f in range(3):
                    packed_k = jnp.where(fours == 8 * f + j, rolled(ha[1 + f, e], 4 * j - offset[side]), packed_k)
            lon_tx[side, v] = packed
            lon_tx[side, 2 + v] = packed_k
        for end, first in enumerate((w, rows)):
            packed = zero
            for i in range(w):
                e = first + i
                packed = jnp.where(in_sample == i, rolled(hx[0, e], 4 * i - offset[side]), packed)
                for f in range(3):
                    packed = jnp.where(fours == 8 * f + 4 + i, rolled(ha[1 + f, e], 16 + 4 * i - offset[side]), packed)
            diag_tx[end, side] = packed

    first_of_two = lax.bitwise_and(lane + 4, 8) != 0
    block_of = lax.bitwise_and(lax.shift_right_logical(lane + LANES - 4, 5), 3)
    for end, first in enumerate((w, rows)):
        for n in range(w // 2):
            e = first + 2 * n
            corner_tx[end, n] = jnp.where(first_of_two, hx[0, e], rolled(hx[0, e + 1], 8))
            packed = zero
            for f in range(3):
                two = jnp.where(first_of_two, ha[1 + f, e], rolled(ha[1 + f, e + 1], 8))
                packed = jnp.where(block_of == f, two, packed)
            corner_tx[end, 2 + n] = packed

    first_lane, last_lane = lane == 0, lane == LANES - 1

    def left(u):
        r0, r1 = pltpu.roll(u[0], 1, 1), pltpu.roll(u[1], 1, 1)
        return [r0, jnp.where(first_lane, r0, r1)]

    def right(u):
        r0, r1 = pltpu.roll(u[0], LANES - 1, 1), pltpu.roll(u[1], LANES - 1, 1)
        return [jnp.where(last_lane, r1, r0), r1]

    def add(*lists):
        lists = [u for u in lists if u is not None]
        total = lists[0]
        for u in lists[1:]:
            total = [p + q for p, q in zip(total, u)]
        return total

    def sub(u, v):
        return [p - q for p, q in zip(u, v)]

    def times(weights, z):
        return [[p * q for p, q in zip(k, z)] if k is not None else None for k in weights]

    def combine(local, above, below, known=None):
        base = add(*[u for u in (known, local and local[0], above and above[1], below and below[1]) if u is not None])
        q3 = sub(above[3], below[3]) if above and below else None
        if local and q3:
            u, v = add(local[2], q3), sub(local[2], q3)
        elif local and above:
            u, v = add(local[2], above[3]), sub(local[2], above[3])
        elif local:
            u, v = sub(local[2], below[3]), add(local[2], below[3])
        elif above:
            return add(base, sub(left(above[3]), right(above[3])))
        else:
            return add(base, sub(right(below[3]), left(below[3])))
        return add(base, add(left(u), right(v)))

    def weights_of(r):
        return [[a[f, r, 0], a[f, r, 1]] for f in range(4)]

    def state(t, s, r):
        return [x[t, s, r, 0], x[t, s, r, 1]]

    def store(t, s, r, value):
        x[t, s, r, 0] = value[0]
        x[t, s, r, 1] = value[1]

    def advance(t, s, first, last):
        def term(r):
            return times(weights_of(r), state(t - 1, s, r))

        above, here = term(first - 1), term(first)
        for r in range(first, last):
            below = term(r + 1)
            store(t, s, r, combine(here, above, below))
            above, here = here, below

    for end in range(2):
        rows_in = (0, 1) if end == 0 else (rows - 1, rows - 2)
        for n, (f, d) in enumerate(((1, 0), (2, 0), (3, 0), (1, 1), (3, 1))):
            for h in range(2):
                k_tx[end, n, h] = a[f, rows_in[d], h]

    def prepare(s, carry):
        advance(1, s, 1, 3)
        advance(1, s, rows - 3, rows - 1)
        for end in range(2):
            row = (lambda d: d) if end == 0 else (lambda d: rows - 1 - d)

            def crossing(term, end=end):
                return combine(None, None, term) if end == 0 else combine(None, term, None)

            def partial(local, inner, end=end):
                return combine(local, None, inner) if end == 0 else combine(local, inner, None)

            t00 = times(weights_of(row(0)), state(0, s, row(0)))
            t01 = times(weights_of(row(1)), state(0, s, row(1)))
            t11 = times(weights_of(row(1)), state(1, s, row(1)))
            t12 = times(weights_of(row(2)), state(1, s, row(2)))
            pieces = (crossing(t00), partial(t00, t01), crossing(t11), partial(t11, t12))
            for n, value in enumerate(pieces):
                for h in range(2):
                    edge_tx[end, s, n, h] = value[h]
        return carry

    lax.fori_loop(0, SAMPLES, prepare, 0)

    for end in range(2):

        @pl.when(jnp.logical_not(present[end]))
        def _(end=end):
            for h in range(2):
                for n in range(5):
                    k_rx[end, n, h] = zero
                for s in range(SAMPLES):
                    for n in range(w):
                        edge_rx[end, s, n, h] = zero
            for side in range(2):
                diag_rx[end, side] = zero
            for n in range(4):
                corner_rx[end, n] = zero

    n_sum = sum(len(group) - 1 for group in groups)
    pl.semaphore_wait(barrier, 2 + n_sum + 3 * has_north.astype(jnp.int32) + 3 * has_south.astype(jnp.int32))

    def remote(src, dst, tx, rx, pa, pb):
        return pltpu.make_async_remote_copy(
            src_ref=src, dst_ref=dst, send_sem=tx, recv_sem=rx, device_id=(pa, pb), device_id_type=MESH
        )

    lon_copies = [
        remote(lon_tx.at[side], lon_rx.at[side], lon_tx_sem.at[side], lon_rx_sem.at[side], ia, (east, west)[side])
        for side in range(2)
    ]
    diag_copies = [
        [
            remote(diag_tx.at[end, side], diag_rx.at[1 - end, side], diag_tx_sem.at[end, side], diag_rx_sem.at[1 - end, side], pa_of[end], (east, west)[side])
            for side in range(2)
        ]
        for end in range(2)
    ]

    def lat_copy(end, piece):
        tx, rx = lat_tx_sem.at[end, piece], lat_rx_sem.at[1 - end, piece]
        if isinstance(piece, int) and piece == SAMPLES:
            return remote(k_tx.at[end], k_rx.at[1 - end], tx, rx, pa_of[end], ib)
        if isinstance(piece, int) and piece == SAMPLES + 1:
            return remote(corner_tx.at[end], corner_rx.at[1 - end], tx, rx, pa_of[end], ib)
        return remote(edge_tx.at[end, piece], edge_rx.at[1 - end, piece], tx, rx, pa_of[end], ib)

    lat_copies = [[lat_copy(end, piece) for piece in range(SAMPLES + 2)] for end in range(2)]

    for end in range(2):

        @pl.when(present[end])
        def _(end=end):
            for c in diag_copies[end]:
                c.start()

    for c in lon_copies:
        c.start()
    for piece in (SAMPLES + 1, SAMPLES, 0, 1, 2, 3):
        for end in range(2):

            @pl.when(present[end])
            def _(end=end, piece=piece):
                lat_copies[end][piece].start()

    def interior(s, carry):
        advance(1, s, 3, rows - 3)
        for t in range(2, ITERS + 1):
            advance(t, s, t, rows - t)
        return carry

    lax.fori_loop(0, SAMPLES, interior, 0)

    for c in lon_copies:
        c.wait_recv()
    from_west, from_east = place < 4, place >= 28
    for v in range(2):
        fw, fe = lon_rx[0, v], lon_rx[1, v]
        for j in range(8):
            e = w + 8 * v + j
            side = jnp.where(from_west, rolled(fw, -4 * j), hx[0, e])
            hx[0, e] = jnp.where(from_east, rolled(fe, 28 - 4 * j), side)
        for f in range(3):
            mine = sample_of == f
            fw = replicate(rolled(jnp.where(mine, lon_rx[0, 2 + v], 0.0), -32 * f))
            fe = replicate(rolled(jnp.where(mine, lon_rx[1, 2 + v], 0.0), -32 * f))
            for j in range(8):
                e = w + 8 * v + j
                side = jnp.where(from_west, rolled(fw, -4 * j), ha[1 + f, e])
                ha[1 + f, e] = jnp.where(from_east, rolled(fe, 28 - 4 * j), side)
    for end, first in enumerate((0, w + rows)):

        @pl.when(present[end])
        def _(end=end):
            for side in range(2):
                diag_copies[1 - end][side].wait_recv()
            lat_copies[1 - end][SAMPLES + 1].wait_recv()

        dw, de = diag_rx[end, 0], diag_rx[end, 1]

        def border(own, fw, fe, i):
            side = jnp.where(from_west, rolled(fw, -4 * i), rolled(own, -8 * (i % 2)))
            return jnp.where(from_east, rolled(fe, 28 - 4 * i), side)

        for i in range(w):
            hx[0, first + i] = border(corner_rx[end, i // 2], dw, de, i)
        for f in range(3):
            mine = jnp.logical_and(sample_of == f, place >= 16)
            fw = replicate(rolled(jnp.where(mine, dw, 0.0), -32 * f - 16))
            fe = replicate(rolled(jnp.where(mine, de, 0.0), -32 * f - 16))
            for n in range(w // 2):
                own = replicate(rolled(jnp.where(block_of == f, corner_rx[end, 2 + n], 0.0), -32 * f))
                for i in (2 * n, 2 * n + 1):
                    ha[1 + f, first + i] = border(own, fw, fe, i)

    def centre(a1, a2):
        return jnp.where(a1 > 0.0, 1.0, 0.0) - 2.0 * (a1 + a2)

    for e in range(tall):
        ha[0, e] = centre(ha[1, e], ha[2, e])
    for t in range(1, ITERS + 1):

        def term(e):
            z = hx[t - 1, e]
            return [ha[f, e] * z for f in range(4)]

        above, here = term(t - 1), term(t)
        for e in range(t, tall - t):
            below = term(e + 1)
            q3 = above[3] - below[3]
            total = here[0] + (above[1] + below[1])
            total = total + pltpu.roll(here[2] + q3, 1, 1)
            hx[t, e] = total + pltpu.roll(here[2] - q3, LANES - 1, 1)
            above, here = here, below

    low_edge, high_edge = lane < 4, lane >= LANES - 4
    for s in range(SAMPLES):
        for r in range(rows):
            side = hx[ITERS, w + r]
            xs[s, r] = jnp.where(low_edge, rolled(side, -32 * s - 4), rolled(side, 100 - 32 * s))
    def finish(s, r, value):
        value = [jnp.where(low_edge, xs[s, r], value[0]), jnp.where(high_edge, xs[s, r], value[1])]
        store(ITERS, s, r, value)
        return [u * u for u in value]

    def wet_sum(total, r, squares):
        for h in range(2):
            v = squares[h] * (1.0 / SAMPLES)
            var[r, h] = v
            total = total + jnp.where(a[1, r, h] > 0.0, v, 0.0)
        return total

    total_v, total_m = zero, zero
    for r in range(rows):
        for h in range(2):
            total_m = total_m + jnp.where(a[1, r, h] > 0.0, 1.0, 0.0)
    for r in range(w, rows - w):
        total_v = wet_sum(total_v, r, add(*[finish(s, r, state(ITERS, s, r)) for s in range(SAMPLES)]))

    for end in range(2):

        @pl.when(present[end])
        def _(end=end):
            lat_copies[1 - end][SAMPLES].wait_recv()

        for h in range(2):
            k_mid[end, h] = centre(k_rx[end, 0, h], k_rx[end, 1, h])

    squares = {}

    def edges(samples):
        for s in samples:
            for end in range(2):

                @pl.when(present[end])
                def _(s=s, end=end):
                    lat_copies[1 - end][s].wait_recv()

        ends = [(end, s) for s in samples for end in range(2)]
        for end, s in ends:
            row = (lambda d: d) if end == 0 else (lambda d: rows - 1 - d)

            def toward(local, outer, inner, known=None, end=end):
                above, below = (outer, inner) if end == 0 else (inner, outer)
                return combine(local, above, below, known)

            def halo(n, end=end):
                return [k_rx[end, n, 0], k_rx[end, n, 1]]

            def known(n, end=end, s=s):
                return [edge_rx[end, s, n, 0], edge_rx[end, s, n, 1]]

            near = [[k_mid[end, 0], k_mid[end, 1]], halo(0), halo(1), halo(2)]
            far = [None, halo(3), None, halo(4)]
            mine = [weights_of(row(d)) for d in range(ITERS + 1)]

            def term(d, value, mine=mine):
                return times(mine[d], value)

            def saved(t, d, row=row, s=s):
                return state(t, s, row(d))

            t0 = [term(d, saved(0, d)) for d in range(2)]
            n1 = toward(None, None, t0[0], known(1))
            y1 = toward(t0[0], None, t0[1], known(0))
            tn = times(near, n1)
            t1 = [term(0, y1), term(1, saved(1, 1)), term(2, saved(1, 2))]
            f2 = toward(None, None, tn, known(3))
            n2 = toward(tn, None, t1[0], known(2))
            y2 = [toward(t1[0], tn, t1[1]), toward(t1[1], t1[0], t1[2])]
            tf, tn = times(far, f2), times(near, n2)
            t2 = [term(0, y2[0]), term(1, y2[1]), term(2, saved(2, 2)), term(3, saved(2, 3))]
            n3 = toward(tn, tf, t2[0])
            y3 = [toward(t2[0], tn, t2[1]), toward(t2[1], t2[0], t2[2]), toward(t2[2], t2[1], t2[3])]
            tn = times(near, n3)
            t3 = [term(d, y3[d]) for d in range(3)] + [term(d, saved(3, d)) for d in (3, 4)]
            for d in range(ITERS):
                value = toward(t3[d], tn if d == 0 else t3[d - 1], t3[d + 1])
                squares.setdefault(row(d), []).append(finish(s, row(d), value))

    edges((0, 1))
    for r in list(squares):
        part_v = add(*squares.pop(r))
        var[r, 0], var[r, 1] = part_v
    edges((2, 3))
    for r in sorted(squares):
        total_v = wet_sum(total_v, r, add([var[r, 0], var[r, 1]], *squares[r]))

    row = lax.broadcasted_iota(jnp.int32, (LEVELS, LANES), 0)
    mine = jnp.where(row == 0, jnp.sum(total_v, axis=0, keepdims=True), jnp.sum(total_m, axis=0, keepdims=True))

    def rank(masks):
        out = 0
        for bit, (ma, mb) in enumerate(masks):
            hit = lax.bitwise_and(ia, ma) + lax.bitwise_and(ib, mb)
            out = out + jnp.where(hit > 0, 1 << bit, 0)
        return out

    def sums(phase, mine):
        group = groups[phase]
        size = len(group)
        me = rank([group[1 << i] for i in range(size.bit_length() - 1)])
        part[phase, me] = mine
        copies = []
        for m in range(1, size):
            ma, mb = group[m]
            pa, pb = lax.bitwise_xor(ia, ma), lax.bitwise_xor(ib, mb)
            slot = part.at[phase, me, pl.ds(0, 2)]
            copies.append(remote(slot, slot, sum_tx_sem.at[phase], sum_rx_sem.at[phase], pa, pb))
            copies[-1].start()

    def all_but_mine(phase):
        slots = part.at[phase, pl.ds(0, len(groups[phase]) - 1), pl.ds(0, 2)]
        return remote(slots, slots, sum_tx_sem.at[phase], sum_rx_sem.at[phase], ia, ib)

    def gather(phase):
        all_but_mine(phase).wait_recv()
        total = part[phase, 0, 0:2]
        for j in range(1, len(groups[phase])):
            total = total + part[phase, j, 0:2]
        return total

    sums(0, mine)
    for r in range(rows):
        for h in range(2):
            wet = jnp.where(a[1, r, h] > 0.0, 1.0, 0.0)
            var[r, h] = wet * lax.rsqrt(jnp.where(wet > 0.0, var[r, h], 1.0) + 1e-06)

    def scaled(s, carry):
        for r in range(rows):
            for h in range(2):
                out[s, h, pl.ds(r, LEVELS, stride=rows), :] = x[ITERS, s, r, h] * var[r, h]
        return carry

    lax.fori_loop(0, SAMPLES, scaled, 0)
    for c in lon_copies:
        c.wait_send()
    for end in range(2):

        @pl.when(present[end])
        def _(end=end):
            for c in diag_copies[end] + lat_copies[end]:
                c.wait_send()

    total = gather(0)
    sums(1, jnp.concatenate([total] * (LEVELS // 2), axis=0))
    for phase in range(2):
        all_but_mine(phase).wait_send()
    total = gather(1)
    both = jnp.sum(total, axis=1, keepdims=True)
    stat[...] = jnp.broadcast_to(both[0:1] / both[1:2], stat.shape)


def scale(field, stat, out, mean, buf, sem):
    copies = [pltpu.make_async_copy(stat, mean, sem.at[SAMPLES, 0])]
    copies[0].start()
    factor = jnp.sqrt(stat[...])
    for s in range(SAMPLES):
        for h in range(2):
            buf[s, h] = field[s, h] * factor
            copies.append(pltpu.make_async_copy(buf.at[s, h], out.at[s, :, pl.ds(h * LANES, LANES)], sem.at[s, h]))
            copies[-1].start()
    for c in copies:
        c.wait()


def bits_of(n):
    return [1 << i for i in range(n.bit_length() - 1)]


def span(masks):
    out = [(0, 0)]
    for ma, mb in masks:
        out += [(x + ma, z + mb) for x, z in out]
    return out


def shards(n_lat, n_lon, noise, diff_lat, diff_lon, shear, sea_mask):
    samples, levels, rows, cols = noise.shape
    lat_bits, lon_bits = bits_of(n_lat), bits_of(n_lon)
    groups = (
        span([(b, 0) for b in lat_bits[:1]] + [(0, b) for b in lon_bits[1:]]),
        span([(b, 0) for b in lat_bits[1:]] + [(0, b) for b in lon_bits[:1]]),
    )
    size = max(len(g) for g in groups)
    tall = rows + 2 * ITERS
    flat = levels * rows
    f32 = jnp.float32
    dma = pltpu.SemaphoreType.DMA
    hbm = pl.BlockSpec(memory_space=pltpu.HBM)
    vmem = pl.BlockSpec(memory_space=pltpu.VMEM)
    field, stat = pl.pallas_call(
        functools.partial(kernel, n_lat, n_lon, rows, groups),
        out_shape=(
            pltpu.VMEM((samples, 2, flat, LANES), f32),
            pltpu.VMEM((1, LANES), f32),
        ),
        in_specs=[hbm] * 5,
        out_specs=(vmem, vmem),
        scratch_shapes=[
            pltpu.VMEM((samples, 2, flat, LANES), f32),
            pltpu.VMEM((3, 2, flat, LANES), f32),
            pltpu.VMEM((2, flat, LANES), jnp.int32),
            pltpu.VMEM((ITERS + 1, samples, rows, 2, levels, LANES), f32),
            pltpu.VMEM((4, rows, 2, levels, LANES), f32),
            pltpu.VMEM((2, samples, ITERS, 2, levels, LANES), f32),
            pltpu.VMEM((2, samples, ITERS, 2, levels, LANES), f32),
            pltpu.VMEM((2, 5, 2, levels, LANES), f32),
            pltpu.VMEM((2, 5, 2, levels, LANES), f32),
            pltpu.VMEM((2, 2, levels, LANES), f32),
            pltpu.VMEM((2, 4, levels, LANES), f32),
            pltpu.VMEM((2, 4, levels, LANES), f32),
            pltpu.VMEM((ITERS + 1, tall, levels, LANES), f32),
            pltpu.VMEM((4, tall, levels, LANES), f32),
            pltpu.VMEM((2, 4, levels, LANES), f32),
            pltpu.VMEM((2, 4, levels, LANES), f32),
            pltpu.VMEM((2, 2, levels, LANES), f32),
            pltpu.VMEM((2, 2, levels, LANES), f32),
            pltpu.VMEM((samples, rows, levels, LANES), f32),
            pltpu.VMEM((rows, 2, levels, LANES), f32),
            pltpu.VMEM((2, size, levels, LANES), f32),
            dma((8, 2)),
            dma((2, samples + 2)),
            dma((2, samples + 2)),
            dma((2,)),
            dma((2,)),
            dma((2, 2)),
            dma((2, 2)),
            dma((2,)),
            dma((2,)),
        ],
        compiler_params=pltpu.CompilerParams(
            collective_id=0, has_side_effects=True, vmem_limit_bytes=60 << 20
        ),
    )(
        noise.reshape(samples, flat, cols),
        diff_lat.reshape(flat, cols),
        diff_lon.reshape(flat, cols),
        shear.reshape(flat, cols),
        sea_mask.reshape(flat, cols),
    )
    out, mean_var = pl.pallas_call(
        scale,
        out_shape=(jax.ShapeDtypeStruct((samples, flat, cols), f32), jax.ShapeDtypeStruct((1, LANES), f32)),
        in_specs=[vmem, vmem],
        out_specs=(hbm, hbm),
        scratch_shapes=[pltpu.VMEM((samples, 2, flat, LANES), f32), dma((samples + 1, 2))],
        compiler_params=pltpu.CompilerParams(vmem_limit_bytes=8 << 20),
    )(pltpu.with_memory_space_constraint(field, pltpu.VMEM), pltpu.with_memory_space_constraint(stat, pltpu.VMEM))
    return out.reshape(noise.shape), mean_var[0, 0]


def solution(mesh):
    return jax.shard_map(
        functools.partial(shards, mesh.shape["lat"], mesh.shape["lon"]),
        mesh=mesh,
        in_specs=(
            P(None, None, "lat", "lon"),
            P(None, "lat", "lon"),
            P(None, "lat", "lon"),
            P(None, "lat", "lon"),
            P(None, "lat", "lon"),
        ),
        out_specs=(P(None, None, "lat", "lon"), P()),
        check_vma=False,
    )
```

time: 30.1 us -> 28.2 us (0.937)
  Pallas kernels: 29.4 us -> 27.4 us
    pallas_call x1, Pallas kernels: 28 us -> 26.5 us  [shards(): pl.pallas_call(functools.partial(kernel, n_lat, n_lon, rows, groups), out...]
    pallas_call x1, Pallas kernels: 1.37 us -> 0.88 us  [shards(): pl.pallas_call(scale, out_shape=(jax.ShapeDtypeStruct((samples, flat, col...]
where the time goes in v3:
time: 28.2 us; the launch traced here: 28 us
  Pallas kernels  27.4 us (97%)
  between operations  0.64 us (2%)
    pallas_call x1, Pallas kernels, shards(): pl.pallas_call(functools.partial(kernel, n_lat, n_lon, rows, groups), out...  26.5 us
    pallas_call x1, Pallas kernels, shards(): pl.pallas_call(scale, out_shape=(jax.ShapeDtypeStruct((samples, flat, col...  0.88 us

profile of v3, /device:TPU:1, one launch (start us, length us, event | category | flops | bytes accessed | tf_op | source)
XLA Modules:
  0.0 28.0 jit_solution(10215120938416667690)
XLA Ops:
  0.6 26.5 %shard_map.68 = (f32[4,2,128,128]{3,2,1,0:T(8,128)S(1)}, f32[1,128]{1,0:T(1,128)S(1)}) custom-call(f32[4,128,256]{2,1,0:T(8,128)} %bitcast.8, f32[128,256]{1,0:T(8,128)} %bitcast.9, f32[128,256]{1,0:T(8,128)} %bitcast.10, f32[128,256]{1,0:T(8,128)} %bitcast.11, s32[128,256]{1,0:T(8,128)} %bitcast.12), custom_call_target="tpu_custom_call" | custom-call | tf_op jit(solution)/shard_map/pallas_call | solution.py:564
  27.1 0.9 %shard_map.69 = (f32[4,128,256]{2,1,0:T(8,128)}, f32[1,128]{1,0:T(1,128)}) custom-call(f32[4,2,128,128]{3,2,1,0:T(8,128)S(1)} %get-tuple-element.6.field, f32[1,128]{1,0:T(1,128)S(1)} %get-tuple-element.7.stat), custom_call_target="tpu_custom_call" | custom-call | tf_op jit(solution)/shard_map/pallas_call | solution.py:614

commit v4 on v3

--- a/solution.py
+++ b/solution.py
@@ -18,7 +18,7 @@
     n_lat, n_lon, rows, groups,
     noise, k_lat, k_lon, shear, sea,
     out, stat,
-    raw, raw_k, raw_m, x, a, edge_tx, edge_rx, k_tx, k_rx, k_mid, corner_tx, corner_rx, hx, ha, lon_tx, lon_rx, diag_tx, diag_rx, xs, var, part,
+    raw, raw_k, raw_m, x, a, edge_tx, edge_rx, k_tx, k_rx, k_mid, echo, corner_tx, corner_rx, hx, ha, lon_tx, lon_rx, diag_tx, diag_rx, xs, var, part,
     in_sem, lat_tx_sem, lat_rx_sem, lon_tx_sem, lon_rx_sem, diag_tx_sem, diag_rx_sem, sum_tx_sem, sum_rx_sem,
 ):
     w = ITERS
@@ -210,29 +210,24 @@
             for h in range(2):
                 k_tx[end, n, h] = a[f, rows_in[d], h]
 
-    def prepare(s, carry):
-        advance(1, s, 1, 3)
-        advance(1, s, rows - 3, rows - 1)
-        for end in range(2):
-            row = (lambda d: d) if end == 0 else (lambda d: rows - 1 - d)
-
-            def crossing(term, end=end):
-                return combine(None, None, term) if end == 0 else combine(None, term, None)
-
-            def partial(local, inner, end=end):
-                return combine(local, None, inner) if end == 0 else combine(local, inner, None)
-
-            t00 = times(weights_of(row(0)), state(0, s, row(0)))
-            t01 = times(weights_of(row(1)), state(0, s, row(1)))
-            t11 = times(weights_of(row(1)), state(1, s, row(1)))
-            t12 = times(weights_of(row(2)), state(1, s, row(2)))
-            pieces = (crossing(t00), partial(t00, t01), crossing(t11), partial(t11, t12))
-            for n, value in enumerate(pieces):
-                for h in range(2):
-                    edge_tx[end, s, n, h] = value[h]
-        return carry
-
-    lax.fori_loop(0, SAMPLES, prepare, 0)
+    pairs = [(end, s) for s in range(SAMPLES) for end in range(2)]
+
+    def row_of(end, d):
+        return d if end == 0 else rows - 1 - d
+
+    def term(t, end, s, d):
+        return times(weights_of(row_of(end, d)), state(t, s, row_of(end, d)))
+
+    def cross(n, end, s, local):
+        value = combine(None, None, local) if end == 0 else combine(None, local, None)
+        for h in range(2):
+            edge_tx[end, n, s, h] = value[h]
+
+    def partial(end, local, inner, outer=None):
+        return combine(local, outer, inner) if end == 0 else combine(local, inner, outer)
+
+    for end, s in pairs:
+        cross(0, end, s, term(0, end, s, 0))
 
     for end in range(2):
 
@@ -243,7 +238,7 @@
                     k_rx[end, n, h] = zero
                 for s in range(SAMPLES):
                     for n in range(w):
-                        edge_rx[end, s, n, h] = zero
+                        edge_rx[end, n, s, h] = zero
             for side in range(2):
                 diag_rx[end, side] = zero
             for n in range(4):
@@ -271,13 +266,13 @@
 
     def lat_copy(end, piece):
         tx, rx = lat_tx_sem.at[end, piece], lat_rx_sem.at[1 - end, piece]
-        if isinstance(piece, int) and piece == SAMPLES:
+        if piece == ITERS:
             return remote(k_tx.at[end], k_rx.at[1 - end], tx, rx, pa_of[end], ib)
-        if isinstance(piece, int) and piece == SAMPLES + 1:
+        if piece == ITERS + 1:
             return remote(corner_tx.at[end], corner_rx.at[1 - end], tx, rx, pa_of[end], ib)
         return remote(edge_tx.at[end, piece], edge_rx.at[1 - end, piece], tx, rx, pa_of[end], ib)
 
-    lat_copies = [[lat_copy(end, piece) for piece in range(SAMPLES + 2)] for end in range(2)]
+    lat_copies = [[lat_copy(end, piece) for piece in range(ITERS + 2)] for end in range(2)]
 
     for end in range(2):
 
@@ -288,12 +283,34 @@
 
     for c in lon_copies:
         c.start()
-    for piece in (SAMPLES + 1, SAMPLES, 0, 1, 2, 3):
+    def send(piece):
         for end in range(2):
 
             @pl.when(present[end])
-            def _(end=end, piece=piece):
+            def _(end=end):
                 lat_copies[end][piece].start()
+
+    send(ITERS + 1)
+    send(0)
+    send(ITERS)
+    alone = {}
+    for end, s in pairs:
+        alone[end, s] = times(weights_of(row_of(end, 0)), partial(end, term(0, end, s, 0), term(0, end, s, 1)))
+        cross(1, end, s, alone[end, s])
+    send(1)
+    for s in range(SAMPLES):
+        advance(1, s, 1, 3)
+        advance(1, s, rows - 3, rows - 1)
+    for end, s in pairs:
+        t10, t11 = alone[end, s], term(1, end, s, 1)
+        t20 = times(weights_of(row_of(end, 0)), partial(end, t10, t11))
+        t21 = times(weights_of(row_of(end, 1)), partial(end, t11, term(1, end, s, 2), t10))
+        alone[end, s] = t20, t21
+        cross(2, end, s, t20)
+    send(2)
+    for end, s in pairs:
+        cross(3, end, s, times(weights_of(row_of(end, 0)), partial(end, *alone[end, s])))
+    send(3)
 
     def interior(s, carry):
         advance(1, s, 3, rows - 3)
@@ -305,45 +322,48 @@
 
     for c in lon_copies:
         c.wait_recv()
-    from_west, from_east = place < 4, place >= 28
+    beyond_edge = jnp.logical_or(place < 4, place >= 28)
+    even_four = lax.bitwise_and(fours, 1) == 0
+    block_before = lax.bitwise_and(lax.shift_right_logical(lane + 4, 5), 3)
+
+    def woven(fw, fe, shift):
+        fe = rolled(fe, shift)
+        return jnp.where(even_four, fw, fe), jnp.where(even_four, fe, fw)
+
     for v in range(2):
-        fw, fe = lon_rx[0, v], lon_rx[1, v]
+        both = woven(lon_rx[0, v], lon_rx[1, v], 28)
         for j in range(8):
             e = w + 8 * v + j
-            side = jnp.where(from_west, rolled(fw, -4 * j), hx[0, e])
-            hx[0, e] = jnp.where(from_east, rolled(fe, 28 - 4 * j), side)
+            hx[0, e] = jnp.where(beyond_edge, rolled(both[j % 2], -4 * j), hx[0, e])
+        both = woven(lon_rx[0, 2 + v], lon_rx[1, 2 + v], -4)
         for f in range(3):
-            mine = sample_of == f
-            fw = replicate(rolled(jnp.where(mine, lon_rx[0, 2 + v], 0.0), -32 * f))
-            fe = replicate(rolled(jnp.where(mine, lon_rx[1, 2 + v], 0.0), -32 * f))
+            even = replicate(jnp.where(block_before == f, both[0], 0.0))
+            odd = replicate(jnp.where(sample_of == f, both[1], 0.0))
             for j in range(8):
                 e = w + 8 * v + j
-                side = jnp.where(from_west, rolled(fw, -4 * j), ha[1 + f, e])
-                ha[1 + f, e] = jnp.where(from_east, rolled(fe, 28 - 4 * j), side)
+                ha[1 + f, e] = jnp.where(beyond_edge, rolled((even, odd)[j % 2], -4 * j), ha[1 + f, e])
     for end, first in enumerate((0, w + rows)):
 
         @pl.when(present[end])
         def _(end=end):
             for side in range(2):
                 diag_copies[1 - end][side].wait_recv()
-            lat_copies[1 - end][SAMPLES + 1].wait_recv()
+            lat_copies[1 - end][ITERS + 1].wait_recv()
 
         dw, de = diag_rx[end, 0], diag_rx[end, 1]
-
-        def border(own, fw, fe, i):
-            side = jnp.where(from_west, rolled(fw, -4 * i), rolled(own, -8 * (i % 2)))
-            return jnp.where(from_east, rolled(fe, 28 - 4 * i), side)
-
+        both = woven(dw, de, 28)
         for i in range(w):
-            hx[0, first + i] = border(corner_rx[end, i // 2], dw, de, i)
+            own = rolled(corner_rx[end, i // 2], -8 * (i % 2))
+            hx[0, first + i] = jnp.where(beyond_edge, rolled(both[i % 2], -4 * i), own)
+        both = woven(dw, de, -4)
         for f in range(3):
-            mine = jnp.logical_and(sample_of == f, place >= 16)
-            fw = replicate(rolled(jnp.where(mine, dw, 0.0), -32 * f - 16))
-            fe = replicate(rolled(jnp.where(mine, de, 0.0), -32 * f - 16))
+            mine = jnp.logical_and(sample_of == f, place >= 12)
+            halves = [replicate(jnp.where(mine, u, 0.0)) for u in both]
             for n in range(w // 2):
-                own = replicate(rolled(jnp.where(block_of == f, corner_rx[end, 2 + n], 0.0), -32 * f))
+                own = replicate(jnp.where(block_of == f, corner_rx[end, 2 + n], 0.0))
                 for i in (2 * n, 2 * n + 1):
-                    ha[1 + f, first + i] = border(own, fw, fe, i)
+                    moved = rolled(halves[i % 2], -16 - 4 * i)
+                    ha[1 + f, first + i] = jnp.where(beyond_edge, moved, rolled(own, -8 * (i % 2)))
 
     def centre(a1, a2):
         return jnp.where(a1 > 0.0, 1.0, 0.0) - 2.0 * (a1 + a2)
@@ -366,10 +386,12 @@
             above, here = here, below
 
     low_edge, high_edge = lane < 4, lane >= LANES - 4
-    for s in range(SAMPLES):
-        for r in range(rows):
-            side = hx[ITERS, w + r]
-            xs[s, r] = jnp.where(low_edge, rolled(side, -32 * s - 4), rolled(side, 100 - 32 * s))
+    for r in range(rows):
+        side = hx[ITERS, w + r]
+        side = jnp.where(place < 4, rolled(side, -24), side)
+        for s in range(SAMPLES):
+            xs[s, r] = rolled(side, -32 * s - 4)
+
     def finish(s, r, value):
         value = [jnp.where(low_edge, xs[s, r], value[0]), jnp.where(high_edge, xs[s, r], value[1])]
         store(ITERS, s, r, value)
@@ -389,74 +411,75 @@
     for r in range(w, rows - w):
         total_v = wet_sum(total_v, r, add(*[finish(s, r, state(ITERS, s, r)) for s in range(SAMPLES)]))
 
+    def arrived(piece):
+        for end in range(2):
+
+            @pl.when(present[end])
+            def _(end=end):
+                lat_copies[1 - end][piece].wait_recv()
+
+    def toward(end, local, outer, inner, known=None):
+        above, below = (outer, inner) if end == 0 else (inner, outer)
+        return combine(local, above, below, known)
+
+    def known(n, end, s):
+        return [edge_rx[end, n, s, 0], edge_rx[end, n, s, 1]]
+
+    def near(end):
+        return [[k_mid[end, 0], k_mid[end, 1]]] + [[k_rx[end, n, 0], k_rx[end, n, 1]] for n in range(3)]
+
+    def far(end):
+        return [None, [k_rx[end, 3, 0], k_rx[end, 3, 1]], None, [k_rx[end, 4, 0], k_rx[end, 4, 1]]]
+
+    def keep(end, s, n, value):
+        echo[end, s, n, 0], echo[end, s, n, 1] = value
+
+    def kept(end, s, n):
+        return [echo[end, s, n, 0], echo[end, s, n, 1]]
+
+    def terms(t, end, s, count):
+        return [times(weights_of(row_of(end, d)), state(t, s, row_of(end, d))) for d in range(count)]
+
+    arrived(0)
+    for end, s in pairs:
+        t0 = terms(0, end, s, 2)
+        keep(end, s, 0, toward(end, None, None, t0[0]))
+        store(1, s, row_of(end, 0), toward(end, t0[0], None, t0[1], known(0, end, s)))
+    arrived(ITERS)
     for end in range(2):
-
-        @pl.when(present[end])
-        def _(end=end):
-            lat_copies[1 - end][SAMPLES].wait_recv()
-
         for h in range(2):
             k_mid[end, h] = centre(k_rx[end, 0, h], k_rx[end, 1, h])
-
+    arrived(1)
+    for end, s in pairs:
+        t1 = terms(1, end, s, 3)
+        beyond = times(near(end), kept(end, s, 0))
+        keep(end, s, 1, toward(end, None, None, beyond))
+        keep(end, s, 0, toward(end, beyond, None, t1[0]))
+        store(2, s, row_of(end, 0), toward(end, t1[0], beyond, t1[1], known(1, end, s)))
+        store(2, s, row_of(end, 1), toward(end, t1[1], t1[0], t1[2]))
+    arrived(2)
+    for end, s in pairs:
+        t2 = terms(2, end, s, 4)
+        beyond = times(near(end), kept(end, s, 0))
+        keep(end, s, 0, toward(end, beyond, times(far(end), kept(end, s, 1)), t2[0]))
+        store(3, s, row_of(end, 0), toward(end, t2[0], beyond, t2[1], known(2, end, s)))
+        for d in (1, 2):
+            store(3, s, row_of(end, d), toward(end, t2[d], t2[d - 1], t2[d + 1]))
     squares = {}
-
-    def edges(samples):
-        for s in samples:
-            for end in range(2):
-
-                @pl.when(present[end])
-                def _(s=s, end=end):
-                    lat_copies[1 - end][s].wait_recv()
-
-        ends = [(end, s) for s in samples for end in range(2)]
-        for end, s in ends:
-            row = (lambda d: d) if end == 0 else (lambda d: rows - 1 - d)
-
-            def toward(local, outer, inner, known=None, end=end):
-                above, below = (outer, inner) if end == 0 else (inner, outer)
-                return combine(local, above, below, known)
-
-            def halo(n, end=end):
-                return [k_rx[end, n, 0], k_rx[end, n, 1]]
-
-            def known(n, end=end, s=s):
-                return [edge_rx[end, s, n, 0], edge_rx[end, s, n, 1]]
-
-            near = [[k_mid[end, 0], k_mid[end, 1]], halo(0), halo(1), halo(2)]
-            far = [None, halo(3), None, halo(4)]
-            mine = [weights_of(row(d)) for d in range(ITERS + 1)]
-
-            def term(d, value, mine=mine):
-                return times(mine[d], value)
-
-            def saved(t, d, row=row, s=s):
-                return state(t, s, row(d))
-
-            t0 = [term(d, saved(0, d)) for d in range(2)]
-            n1 = toward(None, None, t0[0], known(1))
-            y1 = toward(t0[0], None, t0[1], known(0))
-            tn = times(near, n1)
-            t1 = [term(0, y1), term(1, saved(1, 1)), term(2, saved(1, 2))]
-            f2 = toward(None, None, tn, known(3))
-            n2 = toward(tn, None, t1[0], known(2))
-            y2 = [toward(t1[0], tn, t1[1]), toward(t1[1], t1[0], t1[2])]
-            tf, tn = times(far, f2), times(near, n2)
-            t2 = [term(0, y2[0]), term(1, y2[1]), term(2, saved(2, 2)), term(3, saved(2, 3))]
-            n3 = toward(tn, tf, t2[0])
-            y3 = [toward(t2[0], tn, t2[1]), toward(t2[1], t2[0], t2[2]), toward(t2[2], t2[1], t2[3])]
-            tn = times(near, n3)
-            t3 = [term(d, y3[d]) for d in range(3)] + [term(d, saved(3, d)) for d in (3, 4)]
-            for d in range(ITERS):
-                value = toward(t3[d], tn if d == 0 else t3[d - 1], t3[d + 1])
-                squares.setdefault(row(d), []).append(finish(s, row(d), value))
-
-    edges((0, 1))
-    for r in list(squares):
-        part_v = add(*squares.pop(r))
-        var[r, 0], var[r, 1] = part_v
-    edges((2, 3))
+    for end, s in pairs:
+        t3 = terms(3, end, s, 5)
+        beyond = times(near(end), kept(end, s, 0))
+        store(ITERS, s, row_of(end, 0), toward(end, t3[0], beyond, t3[1]))
+        for d in range(1, ITERS):
+            r = row_of(end, d)
+            squares.setdefault(r, []).append(finish(s, r, toward(end, t3[d], t3[d - 1], t3[d + 1])))
     for r in sorted(squares):
-        total_v = wet_sum(total_v, r, add([var[r, 0], var[r, 1]], *squares[r]))
+        total_v = wet_sum(total_v, r, add(*squares[r]))
+    arrived(3)
+    for end in range(2):
+        r = row_of(end, 0)
+        ends = [finish(s, r, add(state(ITERS, s, r), known(3, end, s))) for s in range(SAMPLES)]
+        total_v = wet_sum(total_v, r, add(*ends))
 
     row = lax.broadcasted_iota(jnp.int32, (LEVELS, LANES), 0)
     mine = jnp.where(row == 0, jnp.sum(total_v, axis=0, keepdims=True), jnp.sum(total_m, axis=0, keepdims=True))
@@ -575,11 +598,12 @@
             pltpu.VMEM((2, flat, LANES), jnp.int32),
             pltpu.VMEM((ITERS + 1, samples, rows, 2, levels, LANES), f32),
             pltpu.VMEM((4, rows, 2, levels, LANES), f32),
-            pltpu.VMEM((2, samples, ITERS, 2, levels, LANES), f32),
-            pltpu.VMEM((2, samples, ITERS, 2, levels, LANES), f32),
+            pltpu.VMEM((2, ITERS, samples, 2, levels, LANES), f32),
+            pltpu.VMEM((2, ITERS, samples, 2, levels, LANES), f32),
             pltpu.VMEM((2, 5, 2, levels, LANES), f32),
             pltpu.VMEM((2, 5, 2, levels, LANES), f32),
             pltpu.VMEM((2, 2, levels, LANES), f32),
+            pltpu.VMEM((2, samples, 2, 2, levels, LANES), f32),
             pltpu.VMEM((2, 4, levels, LANES), f32),
             pltpu.VMEM((2, 4, levels, LANES), f32),
             pltpu.VMEM((ITERS + 1, tall, levels, LANES), f32),
@@ -592,8 +616,8 @@
             pltpu.VMEM((rows, 2, levels, LANES), f32),
             pltpu.VMEM((2, size, levels, LANES), f32),
             dma((8, 2)),
-            dma((2, samples + 2)),
-            dma((2, samples + 2)),
+            dma((2, ITERS + 2)),
+            dma((2, ITERS + 2)),
             dma((2,)),
             dma((2,)),
             dma((2, 2)),

time: 28.2 us -> 28 us (level)
  no operation moved by 1% of the time
where the time goes in v4:
time: 28 us; the launch traced here: 27.8 us
  Pallas kernels  27.2 us (97%)
  between operations  0.64 us (2%)
    pallas_call x1, Pallas kernels, shards(): pl.pallas_call(functools.partial(kernel, n_lat, n_lon, rows, groups), out...  26.3 us
    pallas_call x1, Pallas kernels, shards(): pl.pallas_call(scale, out_shape=(jax.ShapeDtypeStruct((samples, flat, col...  0.88 us

profile of v4, /device:TPU:1, one launch (start us, length us, event | category | flops | bytes accessed | tf_op | source)
XLA Modules:
  0.0 27.8 jit_solution(7918263662995795492)
XLA Ops:
  0.6 26.3 %shard_map.68 = (f32[4,2,128,128]{3,2,1,0:T(8,128)S(1)}, f32[1,128]{1,0:T(1,128)S(1)}) custom-call(f32[4,128,256]{2,1,0:T(8,128)} %bitcast.8, f32[128,256]{1,0:T(8,128)} %bitcast.9, f32[128,256]{1,0:T(8,128)} %bitcast.10, f32[128,256]{1,0:T(8,128)} %bitcast.11, s32[128,256]{1,0:T(8,128)} %bitcast.12), custom_call_target="tpu_custom_call" | custom-call | tf_op jit(solution)/shard_map/pallas_call | solution.py:587
  27.0 0.9 %shard_map.69 = (f32[4,128,256]{2,1,0:T(8,128)}, f32[1,128]{1,0:T(1,128)}) custom-call(f32[4,2,128,128]{3,2,1,0:T(8,128)S(1)} %get-tuple-element.6.field, f32[1,128]{1,0:T(1,128)S(1)} %get-tuple-element.7.stat), custom_call_target="tpu_custom_call" | custom-call | tf_op jit(solution)/shard_map/pallas_call | solution.py:638

commit v5 on v4

--- a/solution.py
+++ b/solution.py
@@ -497,7 +497,7 @@
         me = rank([group[1 << i] for i in range(size.bit_length() - 1)])
         part[phase, me] = mine
         copies = []
-        for m in range(1, size):
+        for m in reversed(range(1, size)):
             ma, mb = group[m]
             pa, pb = lax.bitwise_xor(ia, ma), lax.bitwise_xor(ib, mb)
             slot = part.at[phase, me, pl.ds(0, 2)]

time: 28 us -> 27.6 us (0.986)
  Pallas kernels: 27.2 us -> 26.8 us
    pallas_call x1, Pallas kernels: 26.3 us -> 26 us  [shards(): pl.pallas_call(functools.partial(kernel, n_lat, n_lon, rows, groups), out...]
where the time goes in v5:
time: 27.6 us; the launch traced here: 27.5 us
  Pallas kernels  26.8 us (97%)
  between operations  0.64 us (2%)
    pallas_call x1, Pallas kernels, shards(): pl.pallas_call(functools.partial(kernel, n_lat, n_lon, rows, groups), out...  26 us
    pallas_call x1, Pallas kernels, shards(): pl.pallas_call(scale, out_shape=(jax.ShapeDtypeStruct((samples, flat, col...  0.88 us

profile of v5, /device:TPU:1, one launch (start us, length us, event | category | flops | bytes accessed | tf_op | source)
XLA Modules:
  0.0 27.5 jit_solution(4685879536534263408)
XLA Ops:
  0.6 26.0 %shard_map.68 = (f32[4,2,128,128]{3,2,1,0:T(8,128)S(1)}, f32[1,128]{1,0:T(1,128)S(1)}) custom-call(f32[4,128,256]{2,1,0:T(8,128)} %bitcast.8, f32[128,256]{1,0:T(8,128)} %bitcast.9, f32[128,256]{1,0:T(8,128)} %bitcast.10, f32[128,256]{1,0:T(8,128)} %bitcast.11, s32[128,256]{1,0:T(8,128)} %bitcast.12), custom_call_target="tpu_custom_call" | custom-call | tf_op jit(solution)/shard_map/pallas_call | solution.py:587
  26.6 0.9 %shard_map.69 = (f32[4,128,256]{2,1,0:T(8,128)}, f32[1,128]{1,0:T(1,128)}) custom-call(f32[4,2,128,128]{3,2,1,0:T(8,128)S(1)} %get-tuple-element.6.field, f32[1,128]{1,0:T(1,128)S(1)} %get-tuple-element.7.stat), custom_call_target="tpu_custom_call" | custom-call | tf_op jit(solution)/shard_map/pallas_call | solution.py:638

commit v6 on v5

--- a/solution.py
+++ b/solution.py
@@ -61,7 +61,7 @@
     for c in loads:
         c.start()
     for group in groups:
-        for ma, mb in group[1:]:
+        for ma, mb in reversed(group[1:]):
             greet(lax.bitwise_xor(ia, ma), lax.bitwise_xor(ib, mb))
 
     for c in loads[:8]:

time: 27.6 us -> 27.6 us (level)
  no operation moved by 1% of the time
where the time goes in v6:
time: 27.6 us; the launch traced here: 27.5 us
  Pallas kernels  26.9 us (97%)
  between operations  0.64 us (2%)
    pallas_call x1, Pallas kernels, shards(): pl.pallas_call(functools.partial(kernel, n_lat, n_lon, rows, groups), out...  26 us
    pallas_call x1, Pallas kernels, shards(): pl.pallas_call(scale, out_shape=(jax.ShapeDtypeStruct((samples, flat, col...  0.88 us

profile of v6, /device:TPU:1, one launch (start us, length us, event | category | flops | bytes accessed | tf_op | source)
XLA Modules:
  0.0 27.5 jit_solution(5862461483269990618)
XLA Ops:
  0.6 26.0 %shard_map.68 = (f32[4,2,128,128]{3,2,1,0:T(8,128)S(1)}, f32[1,128]{1,0:T(1,128)S(1)}) custom-call(f32[4,128,256]{2,1,0:T(8,128)} %bitcast.8, f32[128,256]{1,0:T(8,128)} %bitcast.9, f32[128,256]{1,0:T(8,128)} %bitcast.10, f32[128,256]{1,0:T(8,128)} %bitcast.11, s32[128,256]{1,0:T(8,128)} %bitcast.12), custom_call_target="tpu_custom_call" | custom-call | tf_op jit(solution)/shard_map/pallas_call | solution.py:587
  26.6 0.9 %shard_map.69 = (f32[4,128,256]{2,1,0:T(8,128)}, f32[1,128]{1,0:T(1,128)}) custom-call(f32[4,2,128,128]{3,2,1,0:T(8,128)S(1)} %get-tuple-element.6.field, f32[1,128]{1,0:T(1,128)S(1)} %get-tuple-element.7.stat), custom_call_target="tpu_custom_call" | custom-call | tf_op jit(solution)/shard_map/pallas_call | solution.py:638

commit v7 on v6

--- a/solution.py
+++ b/solution.py
@@ -61,7 +61,7 @@
     for c in loads:
         c.start()
     for group in groups:
-        for ma, mb in reversed(group[1:]):
+        for _, (ma, mb) in far_first(group):
             greet(lax.bitwise_xor(ia, ma), lax.bitwise_xor(ib, mb))
 
     for c in loads[:8]:
@@ -497,8 +497,7 @@
         me = rank([group[1 << i] for i in range(size.bit_length() - 1)])
         part[phase, me] = mine
         copies = []
-        for m in reversed(range(1, size)):
-            ma, mb = group[m]
+        for _, (ma, mb) in far_first(group):
             pa, pb = lax.bitwise_xor(ia, ma), lax.bitwise_xor(ib, mb)
             slot = part.at[phase, me, pl.ds(0, 2)]
             copies.append(remote(slot, slot, sum_tx_sem.at[phase], sum_rx_sem.at[phase], pa, pb))
@@ -557,6 +556,23 @@
             copies[-1].start()
     for c in copies:
         c.wait()
+
+
+def hops(ma, mb):
+    def apart(p, q, n):
+        return min((p - q) % n, (q - p) % n)
+
+    most = 0
+    for i in range(16):
+        for j in range(16):
+            k, n = i ^ ma, j ^ mb
+            x, other_x = j % 2 * 2 + i // 2 % 2, n % 2 * 2 + k // 2 % 2
+            most = max(most, apart(i // 4, k // 4, 4) + apart(j // 2, n // 2, 8) + apart(x, other_x, 4))
+    return most
+
+
+def far_first(group):
+    return sorted(((hops(*masks), masks) for masks in group[1:]), reverse=True)
 
 
 def bits_of(n):

time: 27.6 us -> 27.5 us (level)
  no operation moved by 1% of the time
where the time goes in v7:
time: 27.5 us; the launch traced here: 27.4 us
  Pallas kernels  26.8 us (97%)
  between operations  0.64 us (2%)
    pallas_call x1, Pallas kernels, shards(): pl.pallas_call(functools.partial(kernel, n_lat, n_lon, rows, groups), out...  25.9 us
    pallas_call x1, Pallas kernels, shards(): pl.pallas_call(scale, out_shape=(jax.ShapeDtypeStruct((samples, flat, col...  0.88 us

profile of v7, /device:TPU:1, one launch (start us, length us, event | category | flops | bytes accessed | tf_op | source)
XLA Modules:
  0.0 27.4 jit_solution(6912106817673878018)
XLA Ops:
  0.6 25.9 %shard_map.68 = (f32[4,2,128,128]{3,2,1,0:T(8,128)S(1)}, f32[1,128]{1,0:T(1,128)S(1)}) custom-call(f32[4,128,256]{2,1,0:T(8,128)} %bitcast.8, f32[128,256]{1,0:T(8,128)} %bitcast.9, f32[128,256]{1,0:T(8,128)} %bitcast.10, f32[128,256]{1,0:T(8,128)} %bitcast.11, s32[128,256]{1,0:T(8,128)} %bitcast.12), custom_call_target="tpu_custom_call" | custom-call | tf_op jit(solution)/shard_map/pallas_call | solution.py:603
  26.5 0.9 %shard_map.69 = (f32[4,128,256]{2,1,0:T(8,128)}, f32[1,128]{1,0:T(1,128)}) custom-call(f32[4,2,128,128]{3,2,1,0:T(8,128)S(1)} %get-tuple-element.6.field, f32[1,128]{1,0:T(1,128)S(1)} %get-tuple-element.7.stat), custom_call_target="tpu_custom_call" | custom-call | tf_op jit(solution)/shard_map/pallas_call | solution.py:654

commit v8 on v7

--- a/solution.py
+++ b/solution.py
@@ -284,9 +284,10 @@
     for c in lon_copies:
         c.start()
     def send(piece):
-        for end in range(2):
-
-            @pl.when(present[end])
+        odd = lax.rem(ia, 2) == 1
+        for end, now in ((1, odd), (0, has_north), (1, jnp.logical_not(odd))):
+
+            @pl.when(jnp.logical_and(present[end], now))
             def _(end=end):
                 lat_copies[end][piece].start()
 

time: 27.5 us -> 27.5 us (level)
  no operation moved by 1% of the time
where the time goes in v8:
time: 27.5 us; the launch traced here: 27.4 us
  Pallas kernels  26.8 us (97%)
  between operations  0.64 us (2%)
    pallas_call x1, Pallas kernels, shards(): pl.pallas_call(functools.partial(kernel, n_lat, n_lon, rows, groups), out...  25.9 us
    pallas_call x1, Pallas kernels, shards(): pl.pallas_call(scale, out_shape=(jax.ShapeDtypeStruct((samples, flat, col...  0.88 us

profile of v8, /device:TPU:1, one launch (start us, length us, event | category | flops | bytes accessed | tf_op | source)
XLA Modules:
  0.0 27.4 jit_solution(11890957167724866326)
XLA Ops:
  0.6 25.9 %shard_map.68 = (f32[4,2,128,128]{3,2,1,0:T(8,128)S(1)}, f32[1,128]{1,0:T(1,128)S(1)}) custom-call(f32[4,128,256]{2,1,0:T(8,128)} %bitcast.8, f32[128,256]{1,0:T(8,128)} %bitcast.9, f32[128,256]{1,0:T(8,128)} %bitcast.10, f32[128,256]{1,0:T(8,128)} %bitcast.11, s32[128,256]{1,0:T(8,128)} %bitcast.12), custom_call_target="tpu_custom_call" | custom-call | tf_op jit(solution)/shard_map/pallas_call | solution.py:604
  26.5 0.9 %shard_map.69 = (f32[4,128,256]{2,1,0:T(8,128)}, f32[1,128]{1,0:T(1,128)}) custom-call(f32[4,2,128,128]{3,2,1,0:T(8,128)S(1)} %get-tuple-element.6.field, f32[1,128]{1,0:T(1,128)S(1)} %get-tuple-element.7.stat), custom_call_target="tpu_custom_call" | custom-call | tf_op jit(solution)/shard_map/pallas_call | solution.py:655
